TPU v7x, 32 devices: a whole 2x2x4 slice. The times are simulated.
32 devices in a mesh: section: 2 (over x), seq: 4 (over y, core), tp: 4 (over z).
Axes of the slice: x: 2, y: 2, z: 4, core: 2. Of those that a mesh axis runs over, the one named last changes fastest.
Arguments:
- hidden_image: bfloat16 [2, 512, 1536], P(None, 'seq'), may hold values from -6 to 6
- hidden_text: bfloat16 [2, 128, 1536], P(None, 'seq'), may hold values from -6 to 6
- latent: float32 [2, 512, 64], P(None, 'seq'), may hold values from -6 to 6
- timestep: int32 [2], replicated, may hold values from 14 to 27
- text_length: int32 [2], replicated, may hold values from 32 to 128, as said below
- text_keep: int32 [2, 128], replicated, may hold values 0 or 1
- patch_order: int32 [4], replicated, may hold values from 0 to 3, each once
- stale_image_kv: bfloat16 [2, 2, 512, 2, 1536], P('section', None, 'seq', None, 'tp'), may hold values from -160 to 160
- stale_text_kv: bfloat16 [2, 2, 128, 2, 1536], P('section', None, 'seq', None, 'tp'), may hold values from -6 to 6
- mod_image: float32 [2, 2, 6, 1536], P('section'), may hold values from -3 to 3
- mod_text: float32 [2, 2, 6, 1536], P('section'), may hold values from -3 to 3
- mod_final: float32 [2, 2, 1536], replicated, may hold values from -3 to 3
- qkv_image: bfloat16 [2, 1536, 3, 1536], P('section', None, None, 'tp'), may hold values from -0.15625 to 0.15625
- out_image: bfloat16 [2, 1536, 1536], P('section', 'tp'), may hold values from -0.15625 to 0.15625
- up_image: bfloat16 [2, 1536, 6144], P('section', None, 'tp'), may hold values from -0.15625 to 0.15625
- down_image: bfloat16 [2, 6144, 1536], P('section', 'tp'), may hold values from -0.078125 to 0.078125
- qkv_text: bfloat16 [2, 1536, 3, 1536], P('section', None, None, 'tp'), may hold values from -0.15625 to 0.15625
- out_text: bfloat16 [2, 1536, 1536], P('section', 'tp'), may hold values from -0.15625 to 0.15625
- up_text: bfloat16 [2, 1536, 6144], P('section', None, 'tp'), may hold values from -0.15625 to 0.15625
- down_text: bfloat16 [2, 6144, 1536], P('section', 'tp'), may hold values from -0.078125 to 0.078125
- final_weight: bfloat16 [1536, 64], replicated, may hold values from -0.3125 to 0.3125
Outputs:
- latent_out: float32 [2, 2, 512, 64], P('section', None, 'seq')
- image_kv_next: bfloat16 [2, 2, 512, 2, 1536], P('section', None, 'seq', None, 'tp')
- text_kv_next: bfloat16 [2, 2, 128, 2, 1536], P('section', None, 'seq', None, 'tp')
- text_hidden: bfloat16 [2, 2, 128, 1536], P('section', None, 'seq')
Inputs may be any that keep to these rules, and one draw needn't show every extreme that they name: `text_length`: some request has exactly 128 text tokens.
All inputs are finite; a program needn't handle non-finite values.
Results may differ from a plain program's by a relative error of at most 0.023.
Values may be sent and summed in bfloat16 or wider, within the bound.
A program may use at most 128 MiB of HBM per device.

v0:
```python
import jax
import jax.numpy as jnp
from jax import lax
from jax.sharding import PartitionSpec as P

HD = 64
STEPS = 28


EPSILON = 1e-06
NEGATIVE = -1e30
TIME_SHIFT = 3.0


def passed_along(value, axis, steps):
    count = lax.axis_size(axis)
    initial, last = (max(0, -steps), min(count, count - steps))
    return lax.ppermute(value, axis, [(source, source + steps) for source in range(initial, last)])


def row_norm(values, shift_rows, scale_rows):
    mean_value = jnp.mean(values, axis=-1, keepdims=True)
    centred = values - mean_value
    variance = jnp.mean(centred * centred, axis=-1, keepdims=True)
    return centred * lax.rsqrt(variance + EPSILON) * (1.0 + scale_rows) + shift_rows


def expand_rows(vectors, row_count):
    return jnp.broadcast_to(
        vectors[:, None, :], (vectors.shape[0], row_count, vectors.shape[1])
    ).reshape(-1, vectors.shape[1])


def project(rows, shift_rows, scale_rows, weight):
    flattened = rows.reshape(-1, rows.shape[-1]).astype(jnp.float32)
    normed = row_norm(flattened, shift_rows, scale_rows).astype(jnp.bfloat16)
    mixed = jnp.dot(
        normed, weight.reshape(weight.shape[0], -1), preferred_element_type=jnp.float32
    ).astype(jnp.bfloat16)
    return mixed.reshape(rows.shape[0], rows.shape[1], 3, -1)


def split_heads(values):
    return values.reshape(values.shape[0], values.shape[1], -1, HD)


def block_scores(queries, keys_block, key_mask):
    scores = jnp.einsum(
        "rqhe,rkhe->rhqk", queries, keys_block, preferred_element_type=jnp.float32
    ) * HD ** (-0.5)
    return jnp.where(key_mask[:, None, None, :], scores, NEGATIVE)


def block_weights(scores, rowmax, values_block, key_mask):
    exponent = jnp.where(key_mask[:, None, None, :], jnp.exp(scores - rowmax[..., None]), 0.0)
    totals = jnp.sum(exponent, axis=-1)
    summed = jnp.einsum(
        "rhqk,rkhe->rhqe",
        exponent.astype(jnp.bfloat16),
        values_block,
        preferred_element_type=jnp.float32,
    )
    return (totals, summed)


def heads_out(totals, summed):
    result = summed / totals[..., None]
    merged = jnp.transpose(result, (0, 2, 1, 3))
    return merged.reshape(result.shape[0], result.shape[2], -1).astype(jnp.bfloat16)


def sigma_of(index_value):
    progress = 1.0 - index_value / STEPS
    return TIME_SHIFT * progress / (1.0 + (TIME_SHIFT - 1.0) * progress)


def on_device(
    hidden_image,
    hidden_text,
    latent,
    timestep,
    text_length,
    text_keep,
    patch_order,
    stale_image_kv,
    stale_text_kv,
    mod_image,
    mod_text,
    mod_final,
    qkv_image,
    out_image,
    up_image,
    down_image,
    qkv_text,
    out_text,
    up_text,
    down_text,
    final_weight,
):
    requests = hidden_image.shape[0]
    model_width = hidden_image.shape[2]
    slot_count = patch_order.shape[0]
    image_local = hidden_image.shape[1]
    text_local = hidden_text.shape[1]
    patch_rows = image_local // slot_count
    group_rows = text_local // slot_count
    slot_rows = patch_rows + group_rows
    local_width = qkv_image.shape[3]
    seq_count = lax.axis_size("seq")
    section_index = lax.axis_index("section")
    first_section = section_index == 0
    text_total = text_keep.shape[1]
    positions = jnp.arange(text_total, dtype=jnp.int32)
    valid_text = (positions[None, :] < text_length[:, None]) & (text_keep == 1)
    stale_image, stale_text = (
        lax.all_gather(stale_image_kv[0], "seq", axis=1, tiled=True),
        lax.all_gather(stale_text_kv[0], "seq", axis=1, tiled=True),
    )
    image_buffer = stale_image.reshape(requests, seq_count, slot_count, patch_rows, 2, local_width)
    text_buffer = stale_text.reshape(requests, seq_count, slot_count, group_rows, 2, local_width)
    image_mrows = [expand_rows(mod_image[0][:, column], patch_rows) for column in range(6)]
    text_mrows = [expand_rows(mod_text[0][:, column], group_rows) for column in range(6)]
    image_input = hidden_image.reshape(requests, slot_count, patch_rows, model_width)
    text_input = hidden_text.reshape(requests, slot_count, group_rows, model_width)
    image_store = jnp.zeros((requests, slot_count, patch_rows, model_width), jnp.bfloat16)
    text_store = jnp.zeros((requests, slot_count, group_rows, model_width), jnp.bfloat16)
    image_kv_store = jnp.zeros((requests, slot_count, patch_rows, 2, local_width), jnp.bfloat16)
    text_kv_store = jnp.zeros((requests, slot_count, group_rows, 2, local_width), jnp.bfloat16)
    arrived_image = jnp.zeros((requests, patch_rows, model_width), jnp.bfloat16)
    arrived_text = jnp.zeros((requests, group_rows, model_width), jnp.bfloat16)
    for moment in range(slot_count + 1):
        slot_raw = moment - section_index
        in_range = (slot_raw >= 0) & (slot_raw < slot_count)
        slot_index = jnp.clip(slot_raw, 0, slot_count - 1)
        patch_index = lax.dynamic_index_in_dim(patch_order, slot_index, 0, keepdims=False)
        image_rows = jnp.where(
            first_section,
            lax.dynamic_index_in_dim(image_input, patch_index, 1, keepdims=False),
            arrived_image,
        )
        text_rows = jnp.where(
            first_section,
            lax.dynamic_index_in_dim(text_input, slot_index, 1, keepdims=False),
            arrived_text,
        )
        image_qkv = project(image_rows, image_mrows[0], image_mrows[1], qkv_image[0])
        text_qkv = project(text_rows, text_mrows[0], text_mrows[1], qkv_text[0])
        fresh_local = jnp.concatenate([image_qkv[:, :, 1:], text_qkv[:, :, 1:]], axis=1)
        queries = split_heads(jnp.concatenate([image_qkv[:, :, 0], text_qkv[:, :, 0]], axis=1))
        fresh_all = lax.all_gather(fresh_local, "seq", axis=1, tiled=True)
        fresh_split = fresh_all.reshape(requests, seq_count, slot_rows, 2, local_width)
        image_buffer = lax.dynamic_update_slice_in_dim(
            image_buffer, fresh_split[:, :, None, :patch_rows], patch_index, axis=2
        )
        text_buffer = lax.dynamic_update_slice_in_dim(
            text_buffer, fresh_split[:, :, None, patch_rows:], slot_index, axis=2
        )
        image_keys = image_buffer.reshape(requests, -1, 2, local_width)
        text_keys = text_buffer.reshape(requests, -1, 2, local_width)
        image_mask = jnp.ones((requests, image_keys.shape[1]), jnp.bool_)
        image_scores = block_scores(queries, split_heads(image_keys[:, :, 0]), image_mask)
        text_scores = block_scores(queries, split_heads(text_keys[:, :, 0]), valid_text)
        rowmax = jnp.maximum(jnp.max(image_scores, axis=-1), jnp.max(text_scores, axis=-1))
        image_totals, image_summed = block_weights(
            image_scores, rowmax, split_heads(image_keys[:, :, 1]), image_mask
        )
        text_totals, text_summed = block_weights(
            text_scores, rowmax, split_heads(text_keys[:, :, 1]), valid_text
        )
        attended = heads_out(image_totals + text_totals, image_summed + text_summed)
        image_part = jnp.dot(
            attended[:, :patch_rows].reshape(-1, local_width),
            out_image[0],
            preferred_element_type=jnp.float32,
        )
        text_part = jnp.dot(
            attended[:, patch_rows:].reshape(-1, local_width),
            out_text[0],
            preferred_element_type=jnp.float32,
        )
        image_flat = image_rows.reshape(-1, model_width).astype(jnp.float32)
        text_flat = text_rows.reshape(-1, model_width).astype(jnp.float32)
        image_sum, text_sum = (
            lax.psum(image_part.astype(jnp.bfloat16), "tp").astype(jnp.float32),
            lax.psum(text_part.astype(jnp.bfloat16), "tp").astype(jnp.float32),
        )
        image_first = image_flat + image_mrows[2] * image_sum
        text_first = text_flat + text_mrows[2] * text_sum
        image_normed = row_norm(image_first, image_mrows[3], image_mrows[4]).astype(jnp.bfloat16)
        text_normed = row_norm(text_first, text_mrows[3], text_mrows[4]).astype(jnp.bfloat16)
        image_hidden = jax.nn.gelu(
            jnp.dot(image_normed, up_image[0], preferred_element_type=jnp.float32), approximate=True
        ).astype(jnp.bfloat16)
        text_hidden_rows = jax.nn.gelu(
            jnp.dot(text_normed, up_text[0], preferred_element_type=jnp.float32), approximate=True
        ).astype(jnp.bfloat16)
        image_down, text_down = (
            lax.psum(
                jnp.dot(image_hidden, down_image[0], preferred_element_type=jnp.float32).astype(
                    jnp.bfloat16
                ),
                "tp",
            ).astype(jnp.float32),
            lax.psum(
                jnp.dot(text_hidden_rows, down_text[0], preferred_element_type=jnp.float32).astype(
                    jnp.bfloat16
                ),
                "tp",
            ).astype(jnp.float32),
        )
        image_new = (image_first + image_mrows[5] * image_down).astype(jnp.bfloat16)
        text_new = (text_first + text_mrows[5] * text_down).astype(jnp.bfloat16)
        image_new_rows = image_new.reshape(requests, patch_rows, model_width)
        text_new_rows = text_new.reshape(requests, group_rows, model_width)
        image_store = jnp.where(
            in_range,
            lax.dynamic_update_index_in_dim(image_store, image_new_rows, patch_index, 1),
            image_store,
        )
        text_store = jnp.where(
            in_range,
            lax.dynamic_update_index_in_dim(text_store, text_new_rows, slot_index, 1),
            text_store,
        )
        image_kv_store = jnp.where(
            in_range,
            lax.dynamic_update_index_in_dim(image_kv_store, image_qkv[:, :, 1:], patch_index, 1),
            image_kv_store,
        )
        text_kv_store = jnp.where(
            in_range,
            lax.dynamic_update_index_in_dim(text_kv_store, text_qkv[:, :, 1:], slot_index, 1),
            text_kv_store,
        )
        if moment < slot_count:
            arrived_image, arrived_text = passed_along(
                (image_new_rows, text_new_rows), "section", 1
            )
    final_rows = image_store.reshape(-1, model_width).astype(jnp.float32)
    final_normed = row_norm(
        final_rows,
        expand_rows(mod_final[:, 0], image_local),
        expand_rows(mod_final[:, 1], image_local),
    ).astype(jnp.bfloat16)
    velocity = jnp.dot(final_normed, final_weight, preferred_element_type=jnp.float32).reshape(
        requests, image_local, -1
    )
    returned = passed_along(velocity.astype(jnp.bfloat16), "section", -1).astype(velocity.dtype)
    velocity_used = jnp.where(first_section, returned, velocity)
    index_value = timestep.astype(jnp.float32)
    sigma_now = sigma_of(index_value)
    sigma_next = sigma_of(index_value + 1.0)
    stepped = latent + (sigma_next - sigma_now)[:, None, None] * velocity_used
    denoised = latent - sigma_now[:, None, None] * velocity_used
    latent_part = jnp.where(first_section, stepped, denoised)[None]
    return (
        latent_part,
        image_kv_store.reshape(requests, image_local, 2, local_width)[None],
        text_kv_store.reshape(requests, text_local, 2, local_width)[None],
        text_store.reshape(requests, text_local, model_width)[None],
    )


def solution(mesh):
    in_specs = (
        P(None, "seq", None),
        P(None, "seq", None),
        P(None, "seq", None),
        P(),
        P(),
        P(),
        P(),
        P("section", None, "seq", None, "tp"),
        P("section", None, "seq", None, "tp"),
        P("section", None, None, None),
        P("section", None, None, None),
        P(),
        P("section", None, None, "tp"),
        P("section", "tp", None),
        P("section", None, "tp"),
        P("section", "tp", None),
        P("section", None, None, "tp"),
        P("section", "tp", None),
        P("section", None, "tp"),
        P("section", "tp", None),
        P(),
    )
    out_specs = (
        P("section", None, "seq", None),
        P("section", None, "seq", None, "tp"),
        P("section", None, "seq", None, "tp"),
        P("section", None, "seq", None),
    )
    return jax.shard_map(
        on_device, mesh=mesh, in_specs=in_specs, out_specs=out_specs, check_vma=False
    )
```

profile of v0, /device:TPU:0, one launch (start us, length us, event | category | flops | bytes accessed | tf_op | source)
XLA Modules:
  0.0 973.7 jit_solution(17814984357155614631)
XLA Ops:
  35.9 8.0 all-gather.1
  44.4 7.1 all_gather.22
  100.5 20.8 %psum.142 = bf16[16,1536]{1,0:T(8,128)(2,1)} all-reduce(bf16[16,1536]{1,0:T(8,128)(2,1)} %convolution_convert_fusion.18), channel_id=1, replica_groups=mesh['section'=2,'seq'=4,'tp'=4] {'tp'}, use_global_device_ids=true, to_apply=%region_14.15 | all-reduce | flops 24576 | bytes 98304 | tf_op jit(solution)/shard_map/psum | solution.py:185
  130.2 17.2 %psum.143 = bf16[16,1536]{1,0:T(8,128)(2,1)} all-reduce(bf16[16,1536]{1,0:T(8,128)(2,1)} %fusion.55), channel_id=1, replica_groups=mesh['section'=2,'seq'=4,'tp'=4] {'tp'}, use_global_device_ids=true, to_apply=%region_17.18 | all-reduce | flops 24576 | bytes 98304 | tf_op jit(solution)/shard_map/psum | solution.py:204
  164.0 24.8 %all-reduce.11.cloned.1.call-done = bf16[64,1536]{1,0:T(8,128)(2,1)} async-done(((bf16[64,1536]{1,0:T(8,128)(2,1)}), bf16[64,1536]{1,0:T(8,128)(2,1)}) %all-reduce.11.cloned.1.call-update) | async-done | bytes 196624 | tf_op jit(solution)/shard_map/psum | solution.py:184
  200.6 33.3 %all-reduce.13.cloned.1.call-done = bf16[64,1536]{1,0:T(8,128)(2,1)} async-done(((bf16[64,1536]{1,0:T(8,128)(2,1)}), bf16[64,1536]{1,0:T(8,128)(2,1)}) %all-reduce.13.cloned.1.call-update) | async-done | bytes 196624 | tf_op jit(solution)/shard_map/psum | solution.py:198
  253.4 7.0 all_gather.24
  291.8 19.2 %psum.146 = bf16[16,1536]{1,0:T(8,128)(2,1)} all-reduce(bf16[16,1536]{1,0:T(8,128)(2,1)} %convolution_convert_fusion.16), channel_id=1, replica_groups=mesh['section'=2,'seq'=4,'tp'=4] {'tp'}, use_global_device_ids=true, to_apply=%region_30.31 | all-reduce | flops 24576 | bytes 98304 | tf_op jit(solution)/shard_map/psum | solution.py:185
  320.1 17.2 %psum.147 = bf16[16,1536]{1,0:T(8,128)(2,1)} all-reduce(bf16[16,1536]{1,0:T(8,128)(2,1)} %fusion.58), channel_id=1, replica_groups=mesh['section'=2,'seq'=4,'tp'=4] {'tp'}, use_global_device_ids=true, to_apply=%region_33.34 | all-reduce | flops 24576 | bytes 98304 | tf_op jit(solution)/shard_map/psum | solution.py:204
  355.5 24.9 %all-reduce.15.cloned.1.call-done = bf16[64,1536]{1,0:T(8,128)(2,1)} async-done(((bf16[64,1536]{1,0:T(8,128)(2,1)}), bf16[64,1536]{1,0:T(8,128)(2,1)}) %all-reduce.15.cloned.1.call-update) | async-done | bytes 196624 | tf_op jit(solution)/shard_map/psum | solution.py:184
  392.5 33.2 %all-reduce.17.cloned.1.call-done = bf16[64,1536]{1,0:T(8,128)(2,1)} async-done(((bf16[64,1536]{1,0:T(8,128)(2,1)}), bf16[64,1536]{1,0:T(8,128)(2,1)}) %all-reduce.17.cloned.1.call-update) | async-done | bytes 196624 | tf_op jit(solution)/shard_map/psum | solution.py:198
  483.8 19.3 %psum.150 = bf16[16,1536]{1,0:T(8,128)(2,1)} all-reduce(bf16[16,1536]{1,0:T(8,128)(2,1)} %convolution_convert_fusion.14), channel_id=1, replica_groups=mesh['section'=2,'seq'=4,'tp'=4] {'tp'}, use_global_device_ids=true, to_apply=%region_46.47 | all-reduce | flops 24576 | bytes 98304 | tf_op jit(solution)/shard_map/psum | solution.py:185
  512.0 17.2 %psum.151 = bf16[16,1536]{1,0:T(8,128)(2,1)} all-reduce(bf16[16,1536]{1,0:T(8,128)(2,1)} %fusion.61), channel_id=1, replica_groups=mesh['section'=2,'seq'=4,'tp'=4] {'tp'}, use_global_device_ids=true, to_apply=%region_49.50 | all-reduce | flops 24576 | bytes 98304 | tf_op jit(solution)/shard_map/psum | solution.py:204
  547.5 24.8 %all-reduce.19.cloned.1.call-done = bf16[64,1536]{1,0:T(8,128)(2,1)} async-done(((bf16[64,1536]{1,0:T(8,128)(2,1)}), bf16[64,1536]{1,0:T(8,128)(2,1)}) %all-reduce.19.cloned.1.call-update) | async-done | bytes 196624 | tf_op jit(solution)/shard_map/psum | solution.py:184
  584.4 33.2 %all-reduce.21.cloned.1.call-done = bf16[64,1536]{1,0:T(8,128)(2,1)} async-done(((bf16[64,1536]{1,0:T(8,128)(2,1)}), bf16[64,1536]{1,0:T(8,128)(2,1)}) %all-reduce.21.cloned.1.call-update) | async-done | bytes 196624 | tf_op jit(solution)/shard_map/psum | solution.py:198
  637.3 7.0 all_gather.26
  675.7 19.2 %psum.154 = bf16[16,1536]{1,0:T(8,128)(2,1)} all-reduce(bf16[16,1536]{1,0:T(8,128)(2,1)} %convolution_convert_fusion.12), channel_id=1, replica_groups=mesh['section'=2,'seq'=4,'tp'=4] {'tp'}, use_global_device_ids=true, to_apply=%region_62.63 | all-reduce | flops 24576 | bytes 98304 | tf_op jit(solution)/shard_map/psum | solution.py:185
  703.9 17.2 %psum.155 = bf16[16,1536]{1,0:T(8,128)(2,1)} all-reduce(bf16[16,1536]{1,0:T(8,128)(2,1)} %fusion.64), channel_id=1, replica_groups=mesh['section'=2,'seq'=4,'tp'=4] {'tp'}, use_global_device_ids=true, to_apply=%region_65.66 | all-reduce | flops 24576 | bytes 98304 | tf_op jit(solution)/shard_map/psum | solution.py:204
  737.7 26.5 %all-reduce.23.cloned.1.call-done = bf16[64,1536]{1,0:T(8,128)(2,1)} async-done(((bf16[64,1536]{1,0:T(8,128)(2,1)}), bf16[64,1536]{1,0:T(8,128)(2,1)}) %all-reduce.23.cloned.1.call-update) | async-done | bytes 196624 | tf_op jit(solution)/shard_map/psum | solution.py:184
  777.7 31.9 %all-reduce.25.cloned.1.call-done = bf16[64,1536]{1,0:T(8,128)(2,1)} async-done(((bf16[64,1536]{1,0:T(8,128)(2,1)}), bf16[64,1536]{1,0:T(8,128)(2,1)}) %all-reduce.25.cloned.1.call-update) | async-done | bytes 196624 | tf_op jit(solution)/shard_map/psum | solution.py:198
  858.6 18.1 %psum.158 = bf16[16,1536]{1,0:T(8,128)(2,1)S(1)} all-reduce(bf16[16,1536]{1,0:T(8,128)(2,1)S(1)} %convolution_convert_fusion.10), channel_id=1, replica_groups=mesh['section'=2,'seq'=4,'tp'=4] {'tp'}, use_global_device_ids=true, to_apply=%region_78.79 | all-reduce | flops 24576 | bytes 98304 | tf_op jit(solution)/shard_map/psum | solution.py:185
  883.4 16.6 %psum.159 = bf16[16,1536]{1,0:T(8,128)(2,1)S(1)} all-reduce(bf16[16,1536]{1,0:T(8,128)(2,1)S(1)} %fusion.67), channel_id=1, replica_groups=mesh['section'=2,'seq'=4,'tp'=4] {'tp'}, use_global_device_ids=true, to_apply=%region_81.82 | all-reduce | flops 24576 | bytes 98304 | tf_op jit(solution)/shard_map/psum | solution.py:204
  900.0 12.1 %all-reduce.27.cloned.1.call-done = bf16[64,1536]{1,0:T(8,128)(2,1)} async-done(((bf16[64,1536]{1,0:T(8,128)(2,1)}), bf16[64,1536]{1,0:T(8,128)(2,1)}) %all-reduce.27.cloned.1.call-update) | async-done | bytes 196624 | tf_op jit(solution)/shard_map/psum | solution.py:184
  923.4 33.2 %all-reduce.29.cloned.1.call-done = bf16[64,1536]{1,0:T(8,128)(2,1)} async-done(((bf16[64,1536]{1,0:T(8,128)(2,1)}), bf16[64,1536]{1,0:T(8,128)(2,1)}) %all-reduce.29.cloned.1.call-update) | async-done | bytes 196624 | tf_op jit(solution)/shard_map/psum | solution.py:198
  (501 shorter events, 459.4 us)
Async XLA Ops:
  7.2 146.5 %copy-start = (bf16[1,384,1536]{2,1,0:T(8,128)(2,1)S(1)}, bf16[1,384,1536]{2,1,0:T(8,128)(2,1)}, u32[]{:S(2)}) copy-start(bf16[1,384,1536]{2,1,0:T(8,128)(2,1)} %param.34) | copy-start | bytes 3538948
  7.2 69.5 %all-gather.4.cloned.1.call-start = ((), (), s32[]{:S(2)}) async-start(), calls=%async_computation.10 | async-start | bytes 1966080 | tf_op jit(solution)/shard_map/all_gather | solution.py:116
  7.9 180.8 %all-reduce.11.cloned.1.call-start = ((), (), s32[]{:S(2)}) async-start(), calls=%async_computation | async-start | bytes 393216 | tf_op jit(solution)/shard_map/psum | solution.py:184
  149.7 6.4 collective-permute-start.1
  155.5 78.3 %all-reduce.13.cloned.1.call-start = ((), (), s32[]{:S(2)}) async-start(), calls=%async_computation.1 | async-start | bytes 393216 | tf_op jit(solution)/shard_map/psum | solution.py:198
  199.1 181.2 %all-reduce.15.cloned.1.call-start = ((), (), s32[]{:S(2)}) async-start(), calls=%async_computation.2 | async-start | bytes 393216 | tf_op jit(solution)/shard_map/psum | solution.py:184
  235.0 6.6 collective-permute-start
  338.8 8.8 collective-permute-start.3
  347.4 78.3 %all-reduce.17.cloned.1.call-start = ((), (), s32[]{:S(2)}) async-start(), calls=%async_computation.3 | async-start | bytes 393216 | tf_op jit(solution)/shard_map/psum | solution.py:198
  391.0 181.3 %all-reduce.19.cloned.1.call-start = ((), (), s32[]{:S(2)}) async-start(), calls=%async_computation.4 | async-start | bytes 393216 | tf_op jit(solution)/shard_map/psum | solution.py:184
  427.0 6.6 collective-permute-start.2
  530.8 8.8 collective-permute-start.5
  539.4 78.3 %all-reduce.21.cloned.1.call-start = ((), (), s32[]{:S(2)}) async-start(), calls=%async_computation.5 | async-start | bytes 393216 | tf_op jit(solution)/shard_map/psum | solution.py:198
  583.0 181.3 %all-reduce.23.cloned.1.call-start = ((), (), s32[]{:S(2)}) async-start(), calls=%async_computation.6 | async-start | bytes 393216 | tf_op jit(solution)/shard_map/psum | solution.py:184
  618.9 6.5 collective-permute-start.4
  722.7 8.9 collective-permute-start.7
  731.3 78.3 %all-reduce.25.cloned.1.call-start = ((), (), s32[]{:S(2)}) async-start(), calls=%async_computation.7 | async-start | bytes 393216 | tf_op jit(solution)/shard_map/psum | solution.py:198
  774.9 137.2 %all-reduce.27.cloned.1.call-start = ((), (), s32[]{:S(2)}) async-start(), calls=%async_computation.8 | async-start | bytes 393216 | tf_op jit(solution)/shard_map/psum | solution.py:184
  810.9 6.6 collective-permute-start.6
  878.2 78.4 %all-reduce.29.cloned.1.call-start = ((), (), s32[]{:S(2)}) async-start(), calls=%async_computation.9 | async-start | bytes 393216 | tf_op jit(solution)/shard_map/psum | solution.py:198
  915.5 41.1 %copy-start.17 = (bf16[64,1536]{1,0:T(8,128)(2,1)S(1)}, bf16[64,1536]{1,0:T(8,128)(2,1)}, u32[]{:S(2)}) copy-start(bf16[64,1536]{1,0:T(8,128)(2,1)} %all-reduce.27.cloned.1.call-done) | copy-start | bytes 589828
  915.5 42.9 %copy-start.51 = (f32[2,1536]{1,0:T(2,128)S(1)}, f32[2,1536]{1,0:T(2,128)}, u32[]{:S(2)}) copy-start(f32[2,1536]{1,0:T(2,128)} %get-tuple-element.117) | copy-start | bytes 36868
  915.5 42.9 %copy-start.52 = (f32[2,1536]{1,0:T(2,128)S(1)}, f32[2,1536]{1,0:T(2,128)}, u32[]{:S(2)}) copy-start(f32[2,1536]{1,0:T(2,128)} %get-tuple-element.118) | copy-start | bytes 36868
  960.1 5.8 collective-permute-start.8
  (55 other events, 485.3 us)
Sparse Core Ops, SparseCore 0:
  9.6 22.3 all-gather.3
  155.6 33.0 all-reduce.10
  199.3 34.5 all-reduce.12
  347.5 32.7 all-reduce.14
  391.2 34.5 all-reduce.16
  539.5 32.7 all-reduce.18
  583.1 34.5 all-reduce.20
  731.4 32.7 all-reduce.22
  775.1 34.5 all-reduce.24
  878.2 33.8 all-reduce.26
  922.0 34.5 all-reduce.28
where the time goes:
time: 988 us; the launch traced here: 974 us
  waiting for transfers between devices  292 us (30%)
  blocking collectives  225 us (23%)
  local copies, waits for them, and re-layouts  159 us (16%)
  matrix products  144 us (15%)
  other arithmetic  92.8 us (9%)
  starting transfers between devices  35.4 us (4%)
  between operations  25.1 us (3%)
    psum x5, waiting for transfers between devices, on_device(): lax.psum(jnp.dot(image_hidden, down_image[0], preferred_element_type=jnp....  165 us
    psum x5, waiting for transfers between devices, on_device(): lax.psum(image_part.astype(jnp.bfloat16), 'tp').astype(jnp.float32)  113 us
    psum x5, blocking collectives, on_device(): lax.psum(text_part.astype(jnp.bfloat16), 'tp').astype(jnp.float32)  96.7 us
    psum x5, blocking collectives, on_device(): lax.psum(jnp.dot(text_hidden_rows, down_text[0], preferred_element_type=j...  85.5 us
    unnamed x148, local copies, waits for them, and re-layouts  43.3 us
    all_gather x5, blocking collectives, on_device(): fresh_all = lax.all_gather(fresh_local, 'seq', axis=1, tiled=True)  35 us
    dot_general x10, matrix products, project(): jnp.dot(normed, weight.reshape(weight.shape[0], -1), preferred_element_ty...  34 us
    ppermute x9, starting transfers between devices, passed_along(): lax.ppermute(value, axis, [(source, source + steps) for source in range(i...  33.8 us
  transfers between devices with their start and end apart: 20, of which 15 were waited for; matrix products, arithmetic and copies ran while one was open for 10% of the time, Pallas kernels for 0%

commit v1 on v0

v1 whole, which is shorter than its diff:
```python
import jax
import jax.numpy as jnp
from jax import lax
from jax.sharding import PartitionSpec as P

HD = 64
STEPS = 28


EPSILON = 1e-06
NEGATIVE = -1e30
TIME_SHIFT = 3.0


def row_norm(values, shift_rows, scale_rows):
    mean_value = jnp.mean(values, axis=-1, keepdims=True)
    centred = values - mean_value
    variance = jnp.mean(centred * centred, axis=-1, keepdims=True)
    return centred * lax.rsqrt(variance + EPSILON) * (1.0 + scale_rows) + shift_rows


def sigma_of(index_value):
    progress = 1.0 - index_value / STEPS
    return TIME_SHIFT * progress / (1.0 + (TIME_SHIFT - 1.0) * progress)


def attend(queries, keys, values, allowed):
    heads = queries.shape[1] // HD
    split = lambda rows: rows.reshape(rows.shape[0], heads, HD)
    scores = jnp.einsum(
        "qhe,khe->hqk", split(queries), split(keys), preferred_element_type=jnp.float32
    ) * HD ** (-0.5)
    scores = jnp.where(allowed[None], scores, NEGATIVE)
    rowmax = jnp.max(scores, axis=-1, keepdims=True)
    exponent = jnp.where(allowed[None], jnp.exp(scores - rowmax), 0.0)
    totals = jnp.sum(exponent, axis=-1)
    summed = jnp.einsum(
        "hqk,khe->hqe",
        exponent.astype(jnp.bfloat16),
        split(values),
        preferred_element_type=jnp.float32,
    )
    result = summed / totals[..., None]
    return jnp.transpose(result, (1, 0, 2)).reshape(queries.shape).astype(jnp.bfloat16)


def allowed_keys(patch_order, live, image_local, text_local, seq_count):
    slot_count = patch_order.shape[0]
    order = jnp.arange(slot_count, dtype=jnp.int32)
    rank = jnp.sum(
        jnp.where(patch_order[:, None] == order[None, :], order[:, None], 0), axis=0
    )
    local = jnp.concatenate(
        [
            jnp.repeat(rank, image_local // slot_count),
            jnp.repeat(order, text_local // slot_count),
        ]
    )
    keys = jnp.tile(local, seq_count)
    fresh = keys[None, :] <= local[:, None]
    kept = jnp.concatenate(
        [
            jnp.ones((live.shape[0], seq_count, image_local), jnp.bool_),
            live.reshape(live.shape[0], seq_count, text_local),
        ],
        axis=2,
    ).reshape(live.shape[0], 1, -1)
    return jnp.concatenate([fresh[None] & kept, ~fresh[None] & kept], axis=2)


def on_device(
    hidden_image,
    hidden_text,
    latent,
    timestep,
    text_length,
    text_keep,
    patch_order,
    stale_image_kv,
    stale_text_kv,
    mod_image,
    mod_text,
    mod_final,
    qkv_image,
    out_image,
    up_image,
    down_image,
    qkv_text,
    out_text,
    up_text,
    down_text,
    final_weight,
):
    requests, image_local, model_width = hidden_image.shape
    text_local = hidden_text.shape[1]
    local_width = qkv_image.shape[3]
    seq_count = lax.axis_size("seq")
    section_index = lax.axis_index("section")
    first_section = section_index == 0
    text_total = text_keep.shape[1]
    positions = jnp.arange(text_total, dtype=jnp.int32)
    live = (positions[None, :] < text_length[:, None]) & (text_keep == 1)
    allowed = allowed_keys(patch_order, live, image_local, text_local, seq_count)
    stale_local = jnp.concatenate(
        [
            stale_image_kv[0].reshape(requests, image_local, 2 * local_width),
            stale_text_kv[0].reshape(requests, text_local, 2 * local_width),
        ],
        axis=1,
    )
    stale = lax.all_gather(stale_local, "seq", axis=1, tiled=True)
    qkv_i = qkv_image[0].reshape(model_width, -1)
    qkv_t = qkv_text[0].reshape(model_width, -1)
    inputs = jnp.concatenate([hidden_image, hidden_text], axis=1)
    arrived = None
    made_rows, made_kv = [], []
    for moment in range(requests + 1):
        request = jnp.clip(moment - section_index, 0, requests - 1)
        pick = lambda values: lax.dynamic_index_in_dim(values, request, 0, keepdims=False)
        rows = inputs[0] if moment == 0 else jnp.where(first_section, pick(inputs), arrived)
        mi, mt = pick(mod_image[0]), pick(mod_text[0])
        image_rows = rows[:image_local].astype(jnp.float32)
        text_rows = rows[image_local:].astype(jnp.float32)
        norm_i = row_norm(image_rows, mi[0], mi[1]).astype(jnp.bfloat16)
        norm_t = row_norm(text_rows, mt[0], mt[1]).astype(jnp.bfloat16)
        dot = lambda left, right: jnp.dot(left, right, preferred_element_type=jnp.float32)
        mixed = jnp.concatenate([dot(norm_i, qkv_i), dot(norm_t, qkv_t)], axis=0).astype(
            jnp.bfloat16
        )
        queries, fresh_local = mixed[:, :local_width], mixed[:, local_width:]
        fresh = lax.all_gather(fresh_local, "seq", axis=0, tiled=True)
        both = jnp.concatenate([fresh, pick(stale)], axis=0)
        attended = attend(
            queries, both[:, :local_width], both[:, local_width:], pick(allowed)
        )
        part = jnp.concatenate(
            [dot(attended[:image_local], out_image[0]), dot(attended[image_local:], out_text[0])],
            axis=0,
        )
        summed = lax.psum(part.astype(jnp.bfloat16), "tp").astype(jnp.float32)
        image_first = image_rows + mi[2] * summed[:image_local]
        text_first = text_rows + mt[2] * summed[image_local:]
        norm_i = row_norm(image_first, mi[3], mi[4]).astype(jnp.bfloat16)
        norm_t = row_norm(text_first, mt[3], mt[4]).astype(jnp.bfloat16)
        act = lambda values: jax.nn.gelu(values, approximate=True).astype(jnp.bfloat16)
        part = jnp.concatenate(
            [
                dot(act(dot(norm_i, up_image[0])), down_image[0]),
                dot(act(dot(norm_t, up_text[0])), down_text[0]),
            ],
            axis=0,
        )
        summed = lax.psum(part.astype(jnp.bfloat16), "tp").astype(jnp.float32)
        new_rows = jnp.concatenate(
            [image_first + mi[5] * summed[:image_local], text_first + mt[5] * summed[image_local:]],
            axis=0,
        ).astype(jnp.bfloat16)
        made_rows.append(new_rows)
        made_kv.append(fresh_local)
        if moment < requests:
            arrived = lax.ppermute(new_rows, "section", [(0, 1)])
    choose = lambda made: jnp.stack(
        [jnp.where(first_section, made[r], made[r + 1]) for r in range(requests)]
    )
    rows_out, kv_out = choose(made_rows), choose(made_kv)
    final_normed = row_norm(
        rows_out[:, :image_local].astype(jnp.float32), mod_final[:, :1], mod_final[:, 1:]
    ).astype(jnp.bfloat16)
    velocity = jnp.dot(
        final_normed.reshape(-1, model_width), final_weight, preferred_element_type=jnp.float32
    ).reshape(requests, image_local, -1)
    returned = lax.ppermute(velocity.astype(jnp.bfloat16), "section", [(1, 0)])
    velocity_used = jnp.where(first_section, returned.astype(velocity.dtype), velocity)
    index_value = timestep.astype(jnp.float32)
    sigma_now = sigma_of(index_value)
    sigma_next = sigma_of(index_value + 1.0)
    stepped = latent + (sigma_next - sigma_now)[:, None, None] * velocity_used
    denoised = latent - sigma_now[:, None, None] * velocity_used
    latent_part = jnp.where(first_section, stepped, denoised)[None]
    return (
        latent_part,
        kv_out[:, :image_local].reshape(requests, image_local, 2, local_width)[None],
        kv_out[:, image_local:].reshape(requests, text_local, 2, local_width)[None],
        rows_out[:, image_local:][None],
    )


def solution(mesh):
    in_specs = (
        P(None, "seq", None),
        P(None, "seq", None),
        P(None, "seq", None),
        P(),
        P(),
        P(),
        P(),
        P("section", None, "seq", None, "tp"),
        P("section", None, "seq", None, "tp"),
        P("section", None, None, None),
        P("section", None, None, None),
        P(),
        P("section", None, None, "tp"),
        P("section", "tp", None),
        P("section", None, "tp"),
        P("section", "tp", None),
        P("section", None, None, "tp"),
        P("section", "tp", None),
        P("section", None, "tp"),
        P("section", "tp", None),
        P(),
    )
    out_specs = (
        P("section", None, "seq", None),
        P("section", None, "seq", None, "tp"),
        P("section", None, "seq", None, "tp"),
        P("section", None, "seq", None),
    )
    return jax.shard_map(
        on_device, mesh=mesh, in_specs=in_specs, out_specs=out_specs, check_vma=False
    )
```

time: 988 us -> 469 us (0.47)
  blocking collectives: 225 us -> 30.6 us
  local copies, waits for them, and re-layouts: 159 us -> 44.8 us
  matrix products: 144 us -> 75.1 us
  waiting for transfers between devices: 292 us -> 238 us
  other arithmetic: 92.8 us -> 46.7 us
  starting transfers between devices: 35.4 us -> 9.25 us
    psum x10 -> x0, blocking collectives: 182 us -> none  [the longest x5 96.7 us: on_device(): lax.psum(text_part.astype(jnp.bfloat16), 'tp').astype(jnp.float32)]
    dot_general x51 -> x22, matrix products: 144 us -> 64.4 us  [the longest x18 51.5 us: on_device(): jnp.dot(left, right, preferred_element_type=jnp.float32)]
    psum x10 -> x6, waiting for transfers between devices: 278 us -> 217 us  [on_device(): summed = lax.psum(part.astype(jnp.bfloat16), 'tp').astype(jnp.float32)]
    slice x52 -> x15, local copies, waits for them, and re-layouts: 71.8 us -> 18.7 us  [the longest x3 6.3 us: on_device(): both[:, local_width:]]
    unnamed x148 -> x119, local copies, waits for them, and re-layouts: 43.3 us -> 16.3 us
    ppermute x9 -> x3, starting transfers between devices: 33.8 us -> 8.33 us  [the longest x2 7.04 us: on_device(): arrived = lax.ppermute(new_rows, 'section', [(0, 1)])]
    select_n x20 -> x3, other arithmetic: 19.9 us -> 1.2 us  [the longest x1 1.09 us: on_device(): jnp.where(first_section, made[r], made[r + 1])]
    concatenate x15 -> x3, local copies, waits for them, and re-layouts: 17.7 us -> 0.04 us  [the longest x1 0.02 us: allowed_keys(): jnp.concatenate([jnp.repeat(rank, image_local // slot_count), jnp.repeat(...]
  transfers between devices with their start and end apart: 20 -> 10, of which waited for: 15 -> 9; matrix products, arithmetic and copies ran while one was open for 10% -> 8% of each run, Pallas kernels for 0% -> 0%
where the time goes in v1:
time: 469 us; the launch traced here: 460 us
  waiting for transfers between devices  238 us (51%)
  matrix products  75.1 us (16%)
  other arithmetic  46.7 us (10%)
  local copies, waits for them, and re-layouts  44.8 us (10%)
  blocking collectives  30.6 us (7%)
  between operations  15.6 us (3%)
  starting transfers between devices  9.25 us (2%)
    psum x6, waiting for transfers between devices, on_device(): summed = lax.psum(part.astype(jnp.bfloat16), 'tp').astype(jnp.float32)  217 us
    dot_general x18, matrix products, on_device(): jnp.dot(left, right, preferred_element_type=jnp.float32)  51.5 us
    all_gather x3, blocking collectives, on_device(): fresh = lax.all_gather(fresh_local, 'seq', axis=0, tiled=True)  30.6 us
    ppermute x2, waiting for transfers between devices, on_device(): arrived = lax.ppermute(new_rows, 'section', [(0, 1)])  17.6 us
    unnamed x119, local copies, waits for them, and re-layouts  16.3 us
    dot_general x3, matrix products, attend(): jnp.einsum('hqk,khe->hqe', exponent.astype(jnp.bfloat16), split(values),...  12.4 us
    sub x3, matrix products, attend(): exponent = jnp.where(allowed[None], jnp.exp(scores - rowmax), 0.0)  10.7 us
  transfers between devices with their start and end apart: 10, of which 9 were waited for; matrix products, arithmetic and copies ran while one was open for 8% of the time, Pallas kernels for 0%

profile of v1, /device:TPU:0, one launch (start us, length us, event | category | flops | bytes accessed | tf_op | source)
XLA Modules:
  0.0 460.4 jit_solution(7927831814289216993)
XLA Ops:
  10.5 6.1 %copy.45 = bf16[1,1536,3,384]{1,3,2,0:T(8,128)(2,1)} copy(bf16[1,1536,3,384]{3,1,2,0:T(8,128)(2,1)} %param.33) | data formatting | bytes 7077888 | tf_op args[12]
  17.1 6.1 %copy.46 = bf16[1,1536,3,384]{1,3,2,0:T(8,128)(2,1)} copy(bf16[1,1536,3,384]{3,1,2,0:T(8,128)(2,1)} %param.37) | data formatting | bytes 7077888 | tf_op args[16]
  34.2 11.1 %all_gather.12 = bf16[640,768]{1,0:T(8,128)(2,1)S(1)} all-gather(bf16[160,768]{1,0:T(8,128)(2,1)S(1)} %pad_maximum_fusion.15), channel_id=1, replica_groups=mesh['section'=2,'seq'=4,'tp'=4] {'seq'}, dimensions={0}, use_global_device_ids=true | all-gather | bytes 1228800 | tf_op jit(solution)/shard_map/all_gather | solution.py:131
  52.9 4.0 fusion.30
  57.0 4.2 fusion.102
  64.8 38.5 %all-reduce.8.cloned.1.call-done = bf16[160,1536]{1,0:T(8,128)(2,1)} async-done(((bf16[160,1536]{1,0:T(8,128)(2,1)}), bf16[160,1536]{1,0:T(8,128)(2,1)}) %all-reduce.8.cloned.1.call-update) | async-done | bytes 491536 | tf_op jit(solution)/shard_map/psum | solution.py:140
  110.2 6.4 %fusion.48 = bf16[128,1536]{1,0:T(8,128)(2,1)} fusion(bf16[1,1536,1536]{2,1,0:T(8,128)(2,1)} %param.36, bf16[1,1536,1536]{2,1,0:T(8,128)(2,1)} %param.35, f32[1536]{0:T(1024)} %get-tuple-element.72, f32[1536]{0:T(1024)} %get-tuple-element.77, f32[128]{0:T(128)} %add_rsqrt_fusion.10, f32[128]{0:T(128)} %copy-done.53, ...), kind=kOutput, calls=%fused_computation.51 | convolution fusion | flops 1211498496 | bytes 11035648 | tf_op jit(solution)/shard_map/dot_general | solution.py:126
  116.6 6.3 %fusion.57 = bf16[32,1536]{1,0:T(8,128)(2,1)} fusion(bf16[1,1536,1536]{2,1,0:T(8,128)(2,1)} %param.40, bf16[1,1536,1536]{2,1,0:T(8,128)(2,1)} %param.39, f32[1536]{0:T(1024)} %get-tuple-element.33, f32[1536]{0:T(1024)} %get-tuple-element.34, f32[32]{0:T(128)} %add_rsqrt_fusion.9, f32[32]{0:T(128)} %copy-done.49, f32[160,1536]{1,0:T(8,128)S(1)} %convert_element_type.188, ...), kind=kOutput, calls=%fused_computation.66 | convolution fusion | flops 302874624 | bytes 9849088 | tf_op jit(solution)/shard_map/dot_general | solution.py:126
  124.8 37.8 %all-reduce.10.cloned.1.call-done = bf16[160,1536]{1,0:T(8,128)(2,1)} async-done(((bf16[160,1536]{1,0:T(8,128)(2,1)}), bf16[160,1536]{1,0:T(8,128)(2,1)}) %all-reduce.10.cloned.1.call-update) | async-done | bytes 491536 | tf_op jit(solution)/shard_map/psum | solution.py:153
  171.2 8.1 %collective-permute-done = bf16[160,1536]{1,0:T(8,128)(2,1)S(1)} collective-permute-done((bf16[160,1536]{1,0:T(8,128)(2,1)S(1)}, bf16[160,1536]{1,0:T(8,128)(2,1)S(1)}, u32[]{:S(2)}, u32[]{:S(2)}) %collective-permute-start) | collective-permute-done | bytes 491552 | tf_op jit(solution)/shard_map/ppermute | solution.py:161
  186.2 9.6 %all_gather.14 = bf16[640,768]{1,0:T(8,128)(2,1)S(1)} all-gather(bf16[160,768]{1,0:T(8,128)(2,1)S(1)} %get-tuple-element.43), channel_id=1, replica_groups=mesh['section'=2,'seq'=4,'tp'=4] {'seq'}, dimensions={0}, use_global_device_ids=true | all-gather | bytes 1228800 | tf_op jit(solution)/shard_map/all_gather | solution.py:131
  212.3 37.5 %all-reduce.12.cloned.1.call-done = bf16[160,1536]{1,0:T(8,128)(2,1)} async-done(((bf16[160,1536]{1,0:T(8,128)(2,1)}), bf16[160,1536]{1,0:T(8,128)(2,1)}) %all-reduce.12.cloned.1.call-update) | async-done | bytes 491536 | tf_op jit(solution)/shard_map/psum | solution.py:140
  251.7 5.5 %fusion.51 = bf16[128,1536]{1,0:T(8,128)(2,1)S(1)} fusion(bf16[1,1536,1536]{2,1,0:T(8,128)(2,1)} %param.36, bf16[1,1536,1536]{2,1,0:T(8,128)(2,1)} %param.35, f32[1536]{0:T(1024)S(1)} %copy-done.47, f32[1536]{0:T(1024)S(1)} %copy-done.48, f32[128]{0:T(128)S(1)} %add_rsqrt_fusion.6, f32[128]{0:T(128)S(1)} %broadcast_multiply_fusion.9, ...), kind=kOutput, calls=%fused_computation.52 | convolution fusion | flops 1211498496 | bytes 11035648 | tf_op jit(solution)/shard_map/dot_general | solution.py:126
  257.2 5.6 %fusion.60 = bf16[32,1536]{1,0:T(8,128)(2,1)S(1)} fusion(bf16[1,1536,1536]{2,1,0:T(8,128)(2,1)} %param.40, bf16[1,1536,1536]{2,1,0:T(8,128)(2,1)} %param.39, f32[1536]{0:T(1024)S(1)} %copy-done.38, f32[1536]{0:T(1024)S(1)} %copy-done.39, f32[32]{0:T(128)S(1)} %add_rsqrt_fusion.5, f32[32]{0:T(128)S(1)} %broadcast_multiply_fusion.3, ...), kind=kOutput, calls=%fused_computation.67 | convolution fusion | flops 302874624 | bytes 9856000 | tf_op jit(solution)/shard_map/dot_general | solution.py:126
  263.8 37.8 %all-reduce.14.cloned.1.call-done = bf16[160,1536]{1,0:T(8,128)(2,1)} async-done(((bf16[160,1536]{1,0:T(8,128)(2,1)}), bf16[160,1536]{1,0:T(8,128)(2,1)}) %all-reduce.14.cloned.1.call-update) | async-done | bytes 491536 | tf_op jit(solution)/shard_map/psum | solution.py:153
  303.2 3.7 collective-permute-start.1
  306.8 9.5 %collective-permute-done.1 = bf16[160,1536]{1,0:T(8,128)(2,1)S(1)} collective-permute-done((bf16[160,1536]{1,0:T(8,128)(2,1)S(1)}, bf16[160,1536]{1,0:T(8,128)(2,1)S(1)}, u32[]{:S(2)}, u32[]{:S(2)}) %collective-permute-start.1) | collective-permute-done | bytes 491552 | tf_op jit(solution)/shard_map/ppermute | solution.py:161
  322.9 9.8 %all_gather.15 = bf16[640,768]{1,0:T(8,128)(2,1)S(1)} all-gather(bf16[160,768]{1,0:T(8,128)(2,1)} %get-tuple-element.41), channel_id=1, replica_groups=mesh['section'=2,'seq'=4,'tp'=4] {'seq'}, dimensions={0}, use_global_device_ids=true | all-gather | bytes 1228800 | tf_op jit(solution)/shard_map/all_gather | solution.py:131
  341.7 4.5 fusion.90
  350.6 36.8 %all-reduce.16.cloned.1.call-done = bf16[160,1536]{1,0:T(8,128)(2,1)} async-done(((bf16[160,1536]{1,0:T(8,128)(2,1)}), bf16[160,1536]{1,0:T(8,128)(2,1)}) %all-reduce.16.cloned.1.call-update) | async-done | bytes 491536 | tf_op jit(solution)/shard_map/psum | solution.py:140
  389.3 6.2 %fusion.54 = bf16[128,1536]{1,0:T(8,128)(2,1)} fusion(bf16[1,1536,1536]{2,1,0:T(8,128)(2,1)} %param.36, bf16[1,1536,1536]{2,1,0:T(8,128)(2,1)} %param.35, f32[1536]{0:T(1024)S(1)} %copy-done.43, f32[1536]{0:T(1024)S(1)} %copy-done.44, f32[128]{0:T(128)S(1)} %add_rsqrt_fusion.2, f32[128]{0:T(128)S(1)} %broadcast_multiply_fusion.7, ...), kind=kOutput, calls=%fused_computation.53 | convolution fusion | flops 1211498496 | bytes 11035648 | tf_op jit(solution)/shard_map/dot_general | solution.py:126
  395.6 6.2 %fusion.63 = bf16[32,1536]{1,0:T(8,128)(2,1)} fusion(bf16[1,1536,1536]{2,1,0:T(8,128)(2,1)} %param.40, bf16[1,1536,1536]{2,1,0:T(8,128)(2,1)} %param.39, f32[1536]{0:T(1024)S(1)} %copy-done.36, f32[1536]{0:T(1024)S(1)} %copy-done.37, f32[32]{0:T(128)S(1)} %add_rsqrt_fusion.1, f32[32]{0:T(128)S(1)} %broadcast_multiply_fusion.1, ...), kind=kOutput, calls=%fused_computation.68 | convolution fusion | flops 302874624 | bytes 9856000 | tf_op jit(solution)/shard_map/dot_general | solution.py:126
  413.0 28.6 %all-reduce.18.cloned.1.call-done = bf16[160,1536]{1,0:T(8,128)(2,1)} async-done(((bf16[160,1536]{1,0:T(8,128)(2,1)}), bf16[160,1536]{1,0:T(8,128)(2,1)}) %all-reduce.18.cloned.1.call-update) | async-done | bytes 491536 | tf_op jit(solution)/shard_map/psum | solution.py:153
  448.6 3.8 collective-permute-done.2
  (279 shorter events, 111.1 us)
Async XLA Ops:
  7.2 55.8 %copy-start = (bf16[1,384,1536]{2,1,0:T(8,128)(2,1)S(1)}, bf16[1,384,1536]{2,1,0:T(8,128)(2,1)}, u32[]{:S(2)}) copy-start(bf16[1,384,1536]{2,1,0:T(8,128)(2,1)} %param.34) | copy-start | bytes 3538948
  7.2 38.1 %all-gather.2.cloned.1.call-start = ((), (), s32[]{:S(2)}) async-start(), calls=%async_computation | async-start | bytes 2457600 | tf_op jit(solution)/shard_map/all_gather | solution.py:111
  10.4 92.8 %all-reduce.8.cloned.1.call-start = ((), (), s32[]{:S(2)}) async-start(), calls=%async_computation.1 | async-start | bytes 983040 | tf_op jit(solution)/shard_map/psum | solution.py:140
  64.5 98.1 %all-reduce.10.cloned.1.call-start = ((), (), s32[]{:S(2)}) async-start(), calls=%async_computation.2 | async-start | bytes 983040 | tf_op jit(solution)/shard_map/psum | solution.py:153
  124.7 125.0 %all-reduce.12.cloned.1.call-start = ((), (), s32[]{:S(2)}) async-start(), calls=%async_computation.3 | async-start | bytes 983040 | tf_op jit(solution)/shard_map/psum | solution.py:140
  166.4 12.9 %collective-permute-start = (bf16[160,1536]{1,0:T(8,128)(2,1)S(1)}, bf16[160,1536]{1,0:T(8,128)(2,1)S(1)}, u32[]{:S(2)}, u32[]{:S(2)}) collective-permute-start(bf16[160,1536]{1,0:T(8,128)(2,1)S(1)} %pad_maximum_fusion.6), channel_id=1, source_target_pairs={{0,16},{1,17},{2,18},{3,19},{4,20},{5,21},{6,22},{7,23},{8,24},{9,... | collective-permute-start | bytes 1474568 | tf_op jit(solution)/shard_map/ppermute | solution.py:161
  185.4 21.2 %copy-start.15 = (bf16[160,768]{1,0:T(8,128)(2,1)}, bf16[160,768]{1,0:T(8,128)(2,1)S(1)}, u32[]{:S(2)}) copy-start(bf16[160,768]{1,0:T(8,128)(2,1)S(1)} %get-tuple-element.43) | copy-start | bytes 737284
  210.3 40.6 %copy-start.28 = (f32[1536]{0:T(1024)S(1)}, f32[1536]{0:T(1024)}, u32[]{:S(2)}) copy-start(f32[1536]{0:T(1024)} %get-tuple-element.78) | copy-start | bytes 18436
  210.3 41.4 %copy-start.47 = (f32[1536]{0:T(1024)S(1)}, f32[1536]{0:T(1024)}, u32[]{:S(2)}) copy-start(f32[1536]{0:T(1024)} %get-tuple-element.70) | copy-start | bytes 18436
  210.3 41.4 %copy-start.48 = (f32[1536]{0:T(1024)S(1)}, f32[1536]{0:T(1024)}, u32[]{:S(2)}) copy-start(f32[1536]{0:T(1024)} %get-tuple-element.82) | copy-start | bytes 18436
  212.0 89.5 %all-reduce.14.cloned.1.call-start = ((), (), s32[]{:S(2)}) async-start(), calls=%async_computation.4 | async-start | bytes 983040 | tf_op jit(solution)/shard_map/psum | solution.py:153
  257.2 45.6 %copy-start.33 = (f32[1536]{0:T(1024)S(1)}, f32[1536]{0:T(1024)}, u32[]{:S(2)}) copy-start(f32[1536]{0:T(1024)} %get-tuple-element.81) | copy-start | bytes 18436
  262.8 40.3 %copy-start.32 = (f32[1536]{0:T(1024)S(1)}, f32[1536]{0:T(1024)}, u32[]{:S(2)}) copy-start(f32[1536]{0:T(1024)} %get-tuple-element.39) | copy-start | bytes 18436
  262.8 54.4 %copy-start.45 = (f32[1536]{0:T(1024)S(1)}, f32[1536]{0:T(1024)}, u32[]{:S(2)}) copy-start(f32[1536]{0:T(1024)} %get-tuple-element.84) | copy-start | bytes 18436
  262.8 54.4 %copy-start.46 = (f32[1536]{0:T(1024)S(1)}, f32[1536]{0:T(1024)}, u32[]{:S(2)}) copy-start(f32[1536]{0:T(1024)} %get-tuple-element.85) | copy-start | bytes 18436
  263.7 123.6 %all-reduce.16.cloned.1.call-start = ((), (), s32[]{:S(2)}) async-start(), calls=%async_computation.5 | async-start | bytes 983040 | tf_op jit(solution)/shard_map/psum | solution.py:140
  303.2 13.2 %collective-permute-start.1 = (bf16[160,1536]{1,0:T(8,128)(2,1)S(1)}, bf16[160,1536]{1,0:T(8,128)(2,1)S(1)}, u32[]{:S(2)}, u32[]{:S(2)}) collective-permute-start(bf16[160,1536]{1,0:T(8,128)(2,1)S(1)} %pad_maximum_fusion.10), channel_id=1, source_target_pairs={{0,16},{1,17},{2,18},{3,19},{4,20},{5,21},{6,22},{7,23},{8,24},{9,... | collective-permute-start | bytes 1474568 | tf_op jit(solution)/shard_map/ppermute | solution.py:161
  346.2 42.3 %copy-start.27 = (f32[1536]{0:T(1024)S(1)}, f32[1536]{0:T(1024)}, u32[]{:S(2)}) copy-start(f32[1536]{0:T(1024)} %get-tuple-element.83) | copy-start | bytes 18436
  346.2 43.1 %copy-start.43 = (f32[1536]{0:T(1024)S(1)}, f32[1536]{0:T(1024)}, u32[]{:S(2)}) copy-start(f32[1536]{0:T(1024)} %get-tuple-element.71) | copy-start | bytes 18436
  346.2 43.1 %copy-start.44 = (f32[1536]{0:T(1024)S(1)}, f32[1536]{0:T(1024)}, u32[]{:S(2)}) copy-start(f32[1536]{0:T(1024)} %get-tuple-element.86) | copy-start | bytes 18436
  349.6 91.9 %all-reduce.18.cloned.1.call-start = ((), (), s32[]{:S(2)}) async-start(), calls=%async_computation.6 | async-start | bytes 983040 | tf_op jit(solution)/shard_map/psum | solution.py:153
  401.8 42.6 %copy-start.10 = (bf16[128,1536]{1,0:T(8,128)(2,1)S(1)}, bf16[128,1536]{1,0:T(8,128)(2,1)}, u32[]{:S(2)}) copy-start(bf16[128,1536]{1,0:T(8,128)(2,1)} %copy-done.9) | copy-start | bytes 1179652
  401.8 42.6 %copy-start.21 = (bf16[32,1536]{1,0:T(8,128)(2,1)S(1)}, bf16[32,1536]{1,0:T(8,128)(2,1)}, u32[]{:S(2)}) copy-start(bf16[32,1536]{1,0:T(8,128)(2,1)} %copy-done.20) | copy-start | bytes 294916
  446.6 5.8 %collective-permute-start.2 = (bf16[2,128,64]{1,2,0:T(8,128)(2,1)S(1)}, bf16[2,128,64]{1,2,0:T(8,128)(2,1)S(1)}, u32[]{:S(2)}, u32[]{:S(2)}) collective-permute-start(bf16[2,128,64]{1,2,0:T(8,128)(2,1)S(1)} %get-tuple-element.68), channel_id=1, source_target_pairs={{16,0},{17,1},{18,2},{19,3},{20,4},{21,5},{22,6},{23,7},{24,8},{25... | collective-permute-start | bytes 98312 | tf_op jit(solution)/shard_map/ppermute | solution.py:172
  (43 other events, 373.5 us)
Sparse Core Ops, SparseCore 0:
  10.6 24.5 all-gather.1
  64.7 38.5 all-reduce.7
  124.8 37.7 all-reduce.9
  212.1 37.5 all-reduce.11
  263.8 37.6 all-reduce.13
  349.8 37.5 all-reduce.15
  403.8 37.6 all-reduce.17

commit v2 on v1

--- a/solution.py
+++ b/solution.py
@@ -1,6 +1,10 @@
+import functools
+
 import jax
 import jax.numpy as jnp
 from jax import lax
+from jax.experimental import pallas as pl
+from jax.experimental.pallas import tpu as pltpu
 from jax.sharding import PartitionSpec as P
 
 HD = 64
@@ -17,6 +21,251 @@
     centred = values - mean_value
     variance = jnp.mean(centred * centred, axis=-1, keepdims=True)
     return centred * lax.rsqrt(variance + EPSILON) * (1.0 + scale_rows) + shift_rows
+
+
+def pack(values):
+    half = values.shape[1] // 2
+    return jnp.concatenate([values[:, :half], values[:, half:]], axis=0).astype(jnp.bfloat16)
+
+
+def unpack(block):
+    wide = block.astype(jnp.float32)
+    rows = wide.shape[0] // 2
+    return jnp.concatenate([wide[:rows], wide[rows:]], axis=1)
+
+
+def finish_kernel(n, image_rows, text_rows, last, *refs):
+    refs = list(refs)
+    take = lambda count: [refs.pop(0) for _ in range(count)]
+    attended, shard, mod = take(3)
+    if not last:
+        following, mod_following = take(2)
+    weights = take(6)
+    if last:
+        (new_shard,) = take(1)
+    else:
+        new_shard, next_normed, next_shard = take(3)
+    held = take(6)
+    part, first, send, arrive, gather, normed_i, normed_t, hidden_i, hidden_t, weight_sems = take(10)
+    send_sems, recv_sems, gather_send_sems, gather_recv_sems = take(4)
+    if not last:
+        passed, passed_to, pass_sems, next_gather = take(4)
+    me = lax.axis_index("tp")
+    section = lax.axis_index("section")
+    loads = [
+        pltpu.make_async_copy(weights[i], held[i], weight_sems.at[i]) for i in range(6)
+    ]
+    for load in loads:
+        load.start()
+    peers = [lax.rem(me + d, n) for d in range(1, n)]
+    barrier = pltpu.get_barrier_semaphore()
+    for peer in peers:
+        pl.semaphore_signal(
+            barrier, inc=1, device_id={"tp": peer}, device_id_type=pl.DeviceIdType.MESH
+        )
+    if not last:
+        pl.semaphore_signal(
+            barrier,
+            inc=1,
+            device_id={"section": 1 - section},
+            device_id_type=pl.DeviceIdType.MESH,
+        )
+    out_i, out_t, up_i, up_t, down_i, down_t = held
+    width = shard.shape[1]
+    step = min(512, width)
+    all_images = image_rows * n
+
+    def product(left_i, left_t, right_i, right_t):
+        @pl.loop(0, width // step)
+        def _(index):
+            columns = pl.ds(pl.multiple_of(index * step, step), step)
+            part[:all_images, columns] = jnp.dot(
+                left_i, right_i[:, columns], preferred_element_type=jnp.float32
+            )
+            part[all_images:, columns] = jnp.dot(
+                left_t, right_t[:, columns], preferred_element_type=jnp.float32
+            )
+
+    def scatter_sum(phase):
+        for j in range(n):
+            send[phase, j] = pack(
+                jnp.concatenate(
+                    [
+                        part[j * image_rows : (j + 1) * image_rows],
+                        part[all_images + j * text_rows : all_images + (j + 1) * text_rows],
+                    ],
+                    axis=0,
+                )
+            )
+        copies = []
+        for d in range(1, n):
+            copies.append(
+                pltpu.make_async_remote_copy(
+                    src_ref=send.at[phase, peers[d - 1]],
+                    dst_ref=arrive.at[phase, d - 1],
+                    send_sem=send_sems.at[phase, d - 1],
+                    recv_sem=recv_sems.at[phase, d - 1],
+                    device_id={"tp": peers[d - 1]},
+                    device_id_type=pl.DeviceIdType.MESH,
+                )
+            )
+            copies[-1].start()
+        total = unpack(send[phase, me])
+        for d in range(1, n):
+            copies[d - 1].wait_recv()
+            total = total + unpack(arrive[phase, d - 1])
+        return total, copies
+
+    def gather_rows(phase, buffer):
+        copies = []
+        for d in range(1, n):
+            copies.append(
+                pltpu.make_async_remote_copy(
+                    src_ref=buffer.at[me],
+                    dst_ref=buffer.at[me],
+                    send_sem=gather_send_sems.at[phase, d - 1],
+                    recv_sem=gather_recv_sems.at[phase, d - 1],
+                    device_id={"tp": peers[d - 1]},
+                    device_id_type=pl.DeviceIdType.MESH,
+                )
+            )
+            copies[-1].start()
+        for copy in copies:
+            copy.wait_recv()
+        return copies
+
+    def both(values, table, function):
+        return jnp.concatenate(
+            [
+                function(values[:image_rows], table[0]),
+                function(values[image_rows:], table[1]),
+            ],
+            axis=0,
+        )
+
+    loads[0].wait()
+    loads[1].wait()
+    product(attended[:all_images], attended[all_images:], out_i, out_t)
+    pl.semaphore_wait(barrier, n - 1 if last else n)
+    total, pending = scatter_sum(0)
+    first[...] = shard[...] + both(total, mod, lambda rows, table: table[2:3] * rows)
+    gather[me] = pack(
+        both(first[...], mod, lambda rows, table: row_norm(rows, table[3:4], table[4:5]))
+    )
+    pending += gather_rows(0, gather)
+    text_parts = []
+    for j in range(n):
+        block = unpack(gather[j])
+        normed_i[j * image_rows : (j + 1) * image_rows] = block[:image_rows].astype(jnp.bfloat16)
+        text_parts.append(block[image_rows:])
+    normed_t[...] = jnp.concatenate(text_parts, axis=0).astype(jnp.bfloat16)
+    loads[2].wait()
+    loads[3].wait()
+
+    @pl.loop(0, up_i.shape[1] // step)
+    def _(index):
+        columns = pl.ds(pl.multiple_of(index * step, step), step)
+        for normed, up, hidden in ((normed_i, up_i, hidden_i), (normed_t, up_t, hidden_t)):
+            hidden[:, columns] = jax.nn.gelu(
+                jnp.dot(normed[...], up[:, columns], preferred_element_type=jnp.float32),
+                approximate=True,
+            ).astype(jnp.bfloat16)
+
+    loads[4].wait()
+    loads[5].wait()
+    product(hidden_i[...], hidden_t[...], down_i, down_t)
+    total, more = scatter_sum(1)
+    pending += more
+    made = (first[...] + both(total, mod, lambda rows, table: table[5:6] * rows)).astype(
+        jnp.bfloat16
+    )
+    new_shard[...] = made
+    if not last:
+        passed[...] = pack(made.astype(jnp.float32))
+        copy = pltpu.make_async_remote_copy(
+            src_ref=passed,
+            dst_ref=passed_to,
+            send_sem=pass_sems.at[0],
+            recv_sem=pass_sems.at[1],
+            device_id={"section": 1 - section},
+            device_id_type=pl.DeviceIdType.MESH,
+        )
+        copy.start()
+        copy.wait_recv()
+        pending.append(copy)
+        next_shard[...] = jnp.where(section == 0, following[...], unpack(passed_to[...]))
+        next_gather[me] = pack(
+            both(
+                next_shard[...],
+                mod_following,
+                lambda rows, table: row_norm(rows, table[0:1], table[1:2]),
+            )
+        )
+        pending += gather_rows(1, next_gather)
+        text_parts = []
+        for j in range(n):
+            block = unpack(next_gather[j])
+            next_normed[j * image_rows : (j + 1) * image_rows] = block[:image_rows].astype(
+                jnp.bfloat16
+            )
+            text_parts.append(block[image_rows:])
+        next_normed[all_images:] = jnp.concatenate(text_parts, axis=0).astype(jnp.bfloat16)
+    for copy in pending:
+        copy.wait_send()
+
+
+def finish(n, attended, shard, mod, following, mod_following, weights):
+    last = following is None
+    rows, width = attended.shape[0], shard.shape[1]
+    shard_rows = shard.shape[0]
+    image_rows = shard_rows * 4 // 5
+    hidden_width = weights[2].shape[1]
+    vmem = pl.BlockSpec(memory_space=pltpu.VMEM)
+    anywhere = pl.BlockSpec(memory_space=pl.ANY)
+    block = (2 * shard_rows, width // 2)
+    bf16, f32 = jnp.bfloat16, jnp.float32
+    operands = [attended, shard, mod] + ([] if last else [following, mod_following])
+    out_shape = [jax.ShapeDtypeStruct((shard_rows, width), bf16)]
+    if not last:
+        out_shape += [
+            jax.ShapeDtypeStruct((rows, width), bf16),
+            jax.ShapeDtypeStruct((shard_rows, width), f32),
+        ]
+    images = image_rows * n
+    texts = rows - images
+    scratch = [pltpu.VMEM(weight.shape, bf16) for weight in weights]
+    scratch += [
+        pltpu.VMEM((rows, width), f32),
+        pltpu.VMEM((shard_rows, width), f32),
+        pltpu.VMEM((2, n) + block, bf16),
+        pltpu.VMEM((2, n - 1) + block, bf16),
+        pltpu.VMEM((n,) + block, bf16),
+        pltpu.VMEM((images, width), bf16),
+        pltpu.VMEM((texts, width), bf16),
+        pltpu.VMEM((images, hidden_width), bf16),
+        pltpu.VMEM((texts, hidden_width), bf16),
+        pltpu.SemaphoreType.DMA((6,)),
+    ]
+    scratch += [pltpu.SemaphoreType.DMA((2, n - 1))] * 4
+    if not last:
+        scratch += [
+            pltpu.VMEM(block, bf16),
+            pltpu.VMEM(block, bf16),
+            pltpu.SemaphoreType.DMA((2,)),
+            pltpu.VMEM((n,) + block, bf16),
+        ]
+    return pl.pallas_call(
+        functools.partial(finish_kernel, n, image_rows, shard_rows - image_rows, last),
+        out_shape=out_shape,
+        in_specs=[vmem] * len(operands) + [anywhere] * 6,
+        out_specs=[vmem] * len(out_shape),
+        scratch_shapes=scratch,
+        compiler_params=pltpu.CompilerParams(
+            collective_id=1 if last else 0,
+            has_side_effects=True,
+            vmem_limit_bytes=48 * 1024 * 1024,
+        ),
+    )(*operands, *weights)
 
 
 def sigma_of(index_value):
@@ -109,68 +358,141 @@
         axis=1,
     )
     stale = lax.all_gather(stale_local, "seq", axis=1, tiled=True)
-    qkv_i = qkv_image[0].reshape(model_width, -1)
-    qkv_t = qkv_text[0].reshape(model_width, -1)
-    inputs = jnp.concatenate([hidden_image, hidden_text], axis=1)
-    arrived = None
-    made_rows, made_kv = [], []
-    for moment in range(requests + 1):
-        request = jnp.clip(moment - section_index, 0, requests - 1)
-        pick = lambda values: lax.dynamic_index_in_dim(values, request, 0, keepdims=False)
-        rows = inputs[0] if moment == 0 else jnp.where(first_section, pick(inputs), arrived)
-        mi, mt = pick(mod_image[0]), pick(mod_text[0])
-        image_rows = rows[:image_local].astype(jnp.float32)
-        text_rows = rows[image_local:].astype(jnp.float32)
-        norm_i = row_norm(image_rows, mi[0], mi[1]).astype(jnp.bfloat16)
-        norm_t = row_norm(text_rows, mt[0], mt[1]).astype(jnp.bfloat16)
+    tp_size = lax.axis_size("tp")
+    shapes_fit = (
+        image_local == 4 * text_local
+        and text_local % (8 * tp_size) == 0
+        and local_width % 128 == 0
+    )
+    if shapes_fit:
+        tp_count = lax.axis_size("tp")
+        qkv_i = qkv_image[0].reshape(model_width, -1)
+        qkv_t = qkv_text[0].reshape(model_width, -1)
+        tp_index = lax.axis_index("tp")
+        image_shard, text_shard = image_local // tp_count, text_local // tp_count
+        shards = jnp.concatenate(
+            [
+                lax.dynamic_slice_in_dim(hidden_image, tp_index * image_shard, image_shard, 1),
+                lax.dynamic_slice_in_dim(hidden_text, tp_index * text_shard, text_shard, 1),
+            ],
+            axis=1,
+        ).astype(jnp.float32)
+        mods = jnp.stack([mod_image[0], mod_text[0]], axis=1)
+        weights = [
+            value[0] for value in (out_image, out_text, up_image, up_text, down_image, down_text)
+        ]
         dot = lambda left, right: jnp.dot(left, right, preferred_element_type=jnp.float32)
-        mixed = jnp.concatenate([dot(norm_i, qkv_i), dot(norm_t, qkv_t)], axis=0).astype(
-            jnp.bfloat16
-        )
-        queries, fresh_local = mixed[:, :local_width], mixed[:, local_width:]
-        fresh = lax.all_gather(fresh_local, "seq", axis=0, tiled=True)
-        both = jnp.concatenate([fresh, pick(stale)], axis=0)
-        attended = attend(
-            queries, both[:, :local_width], both[:, local_width:], pick(allowed)
-        )
-        part = jnp.concatenate(
-            [dot(attended[:image_local], out_image[0]), dot(attended[image_local:], out_text[0])],
-            axis=0,
-        )
-        summed = lax.psum(part.astype(jnp.bfloat16), "tp").astype(jnp.float32)
-        image_first = image_rows + mi[2] * summed[:image_local]
-        text_first = text_rows + mt[2] * summed[image_local:]
-        norm_i = row_norm(image_first, mi[3], mi[4]).astype(jnp.bfloat16)
-        norm_t = row_norm(text_first, mt[3], mt[4]).astype(jnp.bfloat16)
-        act = lambda values: jax.nn.gelu(values, approximate=True).astype(jnp.bfloat16)
-        part = jnp.concatenate(
+
+        def picker(moment):
+            request = jnp.clip(moment - section_index, 0, requests - 1)
+            return lambda values: lax.dynamic_index_in_dim(values, request, 0, keepdims=False)
+
+        shard = shards[0]
+        mod = mods[0]
+        normed = jnp.concatenate(
             [
-                dot(act(dot(norm_i, up_image[0])), down_image[0]),
-                dot(act(dot(norm_t, up_text[0])), down_text[0]),
+                row_norm(hidden_image[0].astype(jnp.float32), mod[0, 0], mod[0, 1]),
+                row_norm(hidden_text[0].astype(jnp.float32), mod[1, 0], mod[1, 1]),
             ],
             axis=0,
-        )
-        summed = lax.psum(part.astype(jnp.bfloat16), "tp").astype(jnp.float32)
-        new_rows = jnp.concatenate(
-            [image_first + mi[5] * summed[:image_local], text_first + mt[5] * summed[image_local:]],
-            axis=0,
         ).astype(jnp.bfloat16)
-        made_rows.append(new_rows)
-        made_kv.append(fresh_local)
-        if moment < requests:
-            arrived = lax.ppermute(new_rows, "section", [(0, 1)])
-    choose = lambda made: jnp.stack(
-        [jnp.where(first_section, made[r], made[r + 1]) for r in range(requests)]
-    )
-    rows_out, kv_out = choose(made_rows), choose(made_kv)
-    final_normed = row_norm(
-        rows_out[:, :image_local].astype(jnp.float32), mod_final[:, :1], mod_final[:, 1:]
-    ).astype(jnp.bfloat16)
-    velocity = jnp.dot(
-        final_normed.reshape(-1, model_width), final_weight, preferred_element_type=jnp.float32
-    ).reshape(requests, image_local, -1)
-    returned = lax.ppermute(velocity.astype(jnp.bfloat16), "section", [(1, 0)])
-    velocity_used = jnp.where(first_section, returned.astype(velocity.dtype), velocity)
+        made_rows, made_kv = [], []
+        for moment in range(requests + 1):
+            pick = picker(moment)
+            mixed = jnp.concatenate(
+                [dot(normed[:image_local], qkv_i), dot(normed[image_local:], qkv_t)], axis=0
+            ).astype(jnp.bfloat16)
+            queries, fresh_local = mixed[:, :local_width], mixed[:, local_width:]
+            fresh = lax.all_gather(fresh_local, "seq", axis=0, tiled=True)
+            both = jnp.concatenate([fresh, pick(stale)], axis=0)
+            attended = attend(queries, both[:, :local_width], both[:, local_width:], pick(allowed))
+            made_kv.append(fresh_local)
+            if moment < requests:
+                following = picker(moment + 1)
+                new_rows, normed, next_shard = finish(
+                    tp_count, attended, shard, mod, following(shards), following(mods), weights
+                )
+                shard, mod = next_shard, following(mods)
+            else:
+                (new_rows,) = finish(tp_count, attended, shard, mod, None, None, weights)
+            made_rows.append(new_rows)
+        choose = lambda made: jnp.stack(
+            [jnp.where(first_section, made[r], made[r + 1]) for r in range(requests)]
+        )
+        shard_out, kv_out = choose(made_rows), choose(made_kv)
+        text_out = lax.all_gather(shard_out[:, image_shard:], "tp", axis=1, tiled=True)
+        final_normed = row_norm(
+            shard_out[:, :image_shard].astype(jnp.float32), mod_final[:, :1], mod_final[:, 1:]
+        ).astype(jnp.bfloat16)
+        velocity = dot(final_normed.reshape(-1, model_width), final_weight).reshape(
+            requests, image_shard, -1
+        )
+        gathered = lax.all_gather(velocity, ("section", "tp"), axis=0)
+        velocity_used = jnp.concatenate(list(gathered[tp_count:]), axis=1)
+    else:
+        qkv_i = qkv_image[0].reshape(model_width, -1)
+        qkv_t = qkv_text[0].reshape(model_width, -1)
+        inputs = jnp.concatenate([hidden_image, hidden_text], axis=1)
+        arrived = None
+        made_rows, made_kv = [], []
+        for moment in range(requests + 1):
+            request = jnp.clip(moment - section_index, 0, requests - 1)
+            pick = lambda values: lax.dynamic_index_in_dim(values, request, 0, keepdims=False)
+            rows = inputs[0] if moment == 0 else jnp.where(first_section, pick(inputs), arrived)
+            mi, mt = pick(mod_image[0]), pick(mod_text[0])
+            image_rows = rows[:image_local].astype(jnp.float32)
+            text_rows = rows[image_local:].astype(jnp.float32)
+            norm_i = row_norm(image_rows, mi[0], mi[1]).astype(jnp.bfloat16)
+            norm_t = row_norm(text_rows, mt[0], mt[1]).astype(jnp.bfloat16)
+            dot = lambda left, right: jnp.dot(left, right, preferred_element_type=jnp.float32)
+            mixed = jnp.concatenate([dot(norm_i, qkv_i), dot(norm_t, qkv_t)], axis=0).astype(
+                jnp.bfloat16
+            )
+            queries, fresh_local = mixed[:, :local_width], mixed[:, local_width:]
+            fresh = lax.all_gather(fresh_local, "seq", axis=0, tiled=True)
+            both = jnp.concatenate([fresh, pick(stale)], axis=0)
+            attended = attend(
+                queries, both[:, :local_width], both[:, local_width:], pick(allowed)
+            )
+            part = jnp.concatenate(
+                [dot(attended[:image_local], out_image[0]), dot(attended[image_local:], out_text[0])],
+                axis=0,
+            )
+            summed = lax.psum(part.astype(jnp.bfloat16), "tp").astype(jnp.float32)
+            image_first = image_rows + mi[2] * summed[:image_local]
+            text_first = text_rows + mt[2] * summed[image_local:]
+            norm_i = row_norm(image_first, mi[3], mi[4]).astype(jnp.bfloat16)
+            norm_t = row_norm(text_first, mt[3], mt[4]).astype(jnp.bfloat16)
+            act = lambda values: jax.nn.gelu(values, approximate=True).astype(jnp.bfloat16)
+            part = jnp.concatenate(
+                [
+                    dot(act(dot(norm_i, up_image[0])), down_image[0]),
+                    dot(act(dot(norm_t, up_text[0])), down_text[0]),
+                ],
+                axis=0,
+            )
+            summed = lax.psum(part.astype(jnp.bfloat16), "tp").astype(jnp.float32)
+            new_rows = jnp.concatenate(
+                [image_first + mi[5] * summed[:image_local], text_first + mt[5] * summed[image_local:]],
+                axis=0,
+            ).astype(jnp.bfloat16)
+            made_rows.append(new_rows)
+            made_kv.append(fresh_local)
+            if moment < requests:
+                arrived = lax.ppermute(new_rows, "section", [(0, 1)])
+        choose = lambda made: jnp.stack(
+            [jnp.where(first_section, made[r], made[r + 1]) for r in range(requests)]
+        )
+        rows_out, kv_out = choose(made_rows), choose(made_kv)
+        final_normed = row_norm(
+            rows_out[:, :image_local].astype(jnp.float32), mod_final[:, :1], mod_final[:, 1:]
+        ).astype(jnp.bfloat16)
+        velocity = jnp.dot(
+            final_normed.reshape(-1, model_width), final_weight, preferred_element_type=jnp.float32
+        ).reshape(requests, image_local, -1)
+        returned = lax.ppermute(velocity.astype(jnp.bfloat16), "section", [(1, 0)])
+        velocity_used = jnp.where(first_section, returned.astype(velocity.dtype), velocity)
+        text_out = rows_out[:, image_local:]
     index_value = timestep.astype(jnp.float32)
     sigma_now = sigma_of(index_value)
     sigma_next = sigma_of(index_value + 1.0)
@@ -181,7 +503,7 @@
         latent_part,
         kv_out[:, :image_local].reshape(requests, image_local, 2, local_width)[None],
         kv_out[:, image_local:].reshape(requests, text_local, 2, local_width)[None],
-        rows_out[:, image_local:][None],
+        text_out[None],
     )
 
 

time: 469 us -> 339 us (0.72); the launches traced: 460 us -> 338 us
  waiting for transfers between devices: 238 us -> 0.04 us
  Pallas kernels: 0 us -> 150 us
  blocking collectives: 30.6 us -> 74.6 us
  matrix products: 75.1 us -> 32.8 us
  other arithmetic: 46.7 us -> 16 us
  starting transfers between devices: 9.25 us -> 0.04 us
    psum x6 -> x0, waiting for transfers between devices: 217 us -> none  [on_device(): summed = lax.psum(part.astype(jnp.bfloat16), 'tp').astype(jnp.float32)]
    pallas_call x0 -> x3, Pallas kernels: none -> 150 us  [finish(): pl.pallas_call(functools.partial(finish_kernel, n, image_rows, shard_rows...]
    all_gather x0 -> x2, blocking collectives: none -> 45 us  [the longest x1 31.4 us: on_device(): gathered = lax.all_gather(velocity, ('section', 'tp'), axis=0)]
    dot_general x18 -> x7, matrix products: 51.5 us -> 9.51 us  [on_device(): jnp.dot(left, right, preferred_element_type=jnp.float32)]
    ppermute x3 -> x0, waiting for transfers between devices: 21.4 us -> none  [the longest x2 17.6 us: on_device(): arrived = lax.ppermute(new_rows, 'section', [(0, 1)])]
    concatenate x11 -> x1, other arithmetic: 8.89 us -> 0.04 us  [on_device(): jnp.concatenate([dot(normed[:image_local], qkv_i), dot(normed[image_local...]
    ppermute x3 -> x0, starting transfers between devices: 8.33 us -> none  [the longest x2 7.04 us: on_device(): arrived = lax.ppermute(new_rows, 'section', [(0, 1)])]
    convert_element_type x6 -> x1, other arithmetic: 6.93 us -> 0.04 us  [on_device(): shards = jnp.concatenate([lax.dynamic_slice_in_dim(hidden_image, tp_index...]
  transfers between devices with their start and end apart: 10 -> 1, of which waited for: 9 -> 0; matrix products, arithmetic and copies ran while one was open for 8% -> 7% of each run, Pallas kernels for 0% -> 0%
where the time goes in v2:
time: 339 us; the launch traced here: 338 us
  Pallas kernels  150 us (44%)
  blocking collectives  74.6 us (22%)
  local copies, waits for them, and re-layouts  49 us (14%)
  matrix products  32.8 us (10%)
  other arithmetic  16 us (5%)
  between operations  14.6 us (4%)
    pallas_call x3, Pallas kernels, finish(): pl.pallas_call(functools.partial(finish_kernel, n, image_rows, shard_rows...  150 us
    all_gather x1, blocking collectives, on_device(): gathered = lax.all_gather(velocity, ('section', 'tp'), axis=0)  31.4 us
    all_gather x3, blocking collectives, on_device(): fresh = lax.all_gather(fresh_local, 'seq', axis=0, tiled=True)  29.5 us
    unnamed x79, local copies, waits for them, and re-layouts  19.3 us
    all_gather x1, blocking collectives, on_device(): lax.all_gather(shard_out[:, image_shard:], 'tp', axis=1, tiled=True)  13.7 us
    dot_general x3, matrix products, attend(): jnp.einsum('hqk,khe->hqe', exponent.astype(jnp.bfloat16), split(values),...  13.2 us
    sub x3, matrix products, attend(): exponent = jnp.where(allowed[None], jnp.exp(scores - rowmax), 0.0)  10.1 us
    dot_general x7, matrix products, on_device(): jnp.dot(left, right, preferred_element_type=jnp.float32)  9.51 us
  transfers between devices with their start and end apart: 1, of which 0 were waited for; matrix products, arithmetic and copies ran while one was open for 7% of the time, Pallas kernels for 0%

profile of v2, /device:TPU:0, one launch (start us, length us, event | category | flops | bytes accessed | tf_op | source)
XLA Modules:
  0.0 337.5 jit_solution(10285625440027490585)
XLA Ops:
  11.5 6.2 %copy.82 = bf16[1,1536,3,384]{1,3,2,0:T(8,128)(2,1)} copy(bf16[1,1536,3,384]{3,1,2,0:T(8,128)(2,1)} %param.33) | data formatting | bytes 7077888 | tf_op args[12]
  18.1 6.1 %copy.83 = bf16[1,1536,3,384]{1,3,2,0:T(8,128)(2,1)} copy(bf16[1,1536,3,384]{3,1,2,0:T(8,128)(2,1)} %param.37) | data formatting | bytes 7077888 | tf_op args[16]
  24.6 3.5 %convolution_convert_fusion.2 = bf16[128,1152]{1,0:T(8,128)(2,1)S(1)} fusion(bf16[1536,1152]{0,1:T(8,128)(2,1)} %bitcast.163, f32[1536]{0:T(1024)S(1)} %get-tuple-element.35, f32[1536]{0:T(1024)S(1)} %get-tuple-element.32, f32[128]{0:T(128)S(1)} %add_rsqrt_fusion.2, f32[128]{0:T(128)S(1)} %broadcast_multiply_fusion.2, bf16[2,128,1536]{2,1,0:T(8,128)(2,1)S(1)} %copy-done.20), kind=kOutput, calls=%fused_computation.29 | convolution fusion | flops 454311936 | bytes 4244480 | tf_op jit(solution)/shard_map/dot_general | solution.py:384
  33.6 11.3 %all_gather.18 = bf16[640,768]{1,0:T(8,128)(2,1)S(1)} all-gather(bf16[160,768]{1,0:T(8,128)(2,1)S(1)} %pad_maximum_fusion.6), channel_id=1, replica_groups=mesh['section'=2,'seq'=4,'tp'=4] {'seq'}, dimensions={0}, use_global_device_ids=true | all-gather | bytes 1228800 | tf_op jit(solution)/shard_map/all_gather | solution.py:406
  45.7 3.3 dynamic-slice_bitcast_fusion
  53.1 3.1 fusion.6
  56.3 4.6 %fusion.48 = bf16[160,6,64]{0,2,1:T(8,128)(2,1)} fusion(bf16[1280,6,64]{0,2,1:T(8,128)(2,1)} %bitcast.173, pred[160,1280]{1,0:T(8,128)(4,1)} %copy-done.26, f32[160,6]{0,1:T(8,128)S(1)} %bitcast.185, bf16[160,6,64]{0,2,1:T(8,128)(2,1)} %bitcast.177, bf16[1280,6,64]{0,2,1:T(8,128)(2,1)} %bitcast.169), kind=kOutput, calls=%fused_computation.53 | convolution fusion | flops 320841920 | bytes 2420480 | tf_op jit(solution)/shard_map/hqk,khe->hqe/dot_general | solution.py:286
  64.4 54.3 %shard_map.228 = (bf16[40,1536]{1,0:T(8,128)(2,1)S(1)}, bf16[160,1536]{1,0:T(8,128)(2,1)S(1)}, f32[40,1536]{1,0:T(8,128)S(1)}) custom-call(bf16[160,384]{1,0:T(8,128)(2,1)S(1)} %copy-done.5, f32[40,1536]{1,0:T(8,128)S(1)} %get-tuple-element.55.refs_1_, f32[2,6,1536]{2,1,0:T(8,128)S(1)} %copy-done.4, f32[40,1536]{1,0:T(8,128)S(1)} %get-tuple-element.54.refs_3_, ...), custom_call_target="tpu_custom_call" | custom-call | tf_op jit(solution)/shard_map/pallas_call | solution.py:257
  126.4 9.5 %all_gather.20 = bf16[640,768]{1,0:T(8,128)(2,1)S(1)} all-gather(bf16[160,768]{1,0:T(8,128)(2,1)S(1)} %get-tuple-element.39), channel_id=1, replica_groups=mesh['section'=2,'seq'=4,'tp'=4] {'seq'}, dimensions={0}, use_global_device_ids=true | all-gather | bytes 1228800 | tf_op jit(solution)/shard_map/all_gather | solution.py:406
  135.9 2.6 fusion.52
  138.5 2.3 copy.89
  140.8 2.3 copy.90
  143.1 3.4 %fusion.8 = f32[6,160]{1,0:T(8,128)S(1)} fusion(pred[160,1280]{1,0:T(8,128)(4,1)S(1)} %copy-done.25, bf16[160,6,64]{0,2,1:T(8,128)(2,1)S(1)} %bitcast.178, bf16[1280,6,64]{0,2,1:T(8,128)(2,1)} %bitcast.170), kind=kOutput, calls=%fused_computation.14 | convolution fusion | flops 163431680 | bytes 1314560 | tf_op jit(solution)/shard_map/sub | solution.py:284
  146.5 4.3 %fusion.42 = bf16[160,6,64]{0,2,1:T(8,128)(2,1)} fusion(bf16[1280,6,64]{0,2,1:T(8,128)(2,1)} %bitcast.174, pred[160,1280]{1,0:T(8,128)(4,1)S(1)} %copy-done.25, f32[160,6]{0,1:T(8,128)S(1)} %bitcast.186, bf16[160,6,64]{0,2,1:T(8,128)(2,1)S(1)} %bitcast.179, bf16[1280,6,64]{0,2,1:T(8,128)(2,1)} %bitcast.171), kind=kOutput, calls=%fused_computation.51 | convolution fusion | flops 320841920 | bytes 2420480 | tf_op jit(solution)/shard_map/hqk,khe->hqe/dot_general | solution.py:286
  152.8 56.1 %shard_map.229 = (bf16[40,1536]{1,0:T(8,128)(2,1)S(1)}, bf16[160,1536]{1,0:T(8,128)(2,1)S(1)}, f32[40,1536]{1,0:T(8,128)S(1)}) custom-call(bf16[160,384]{1,0:T(8,128)(2,1)S(1)} %copy.91.refs_0_, f32[40,1536]{1,0:T(8,128)S(1)} %copy-done.7, f32[2,6,1536]{2,1,0:T(8,128)S(1)} %get-tuple-element.65.refs_4_.refs_2_, f32[40,1536]{1,0:T(8,128)S(1)} %get-tuple-element.53.refs_3_, ...), custom_call_target="tpu_custom_call" | custom-call | tf_op jit(solution)/shard_map/pallas_call | solution.py:257
  214.3 8.7 %all_gather.21 = bf16[640,768]{1,0:T(8,128)(2,1)S(1)} all-gather(bf16[160,768]{1,0:T(8,128)(2,1)} %get-tuple-element.37), channel_id=1, replica_groups=mesh['section'=2,'seq'=4,'tp'=4] {'seq'}, dimensions={0}, use_global_device_ids=true | all-gather | bytes 1228800 | tf_op jit(solution)/shard_map/all_gather | solution.py:406
  223.0 2.7 fusion.51
  225.6 2.3 copy.93
  227.9 2.3 copy.94
  230.2 3.5 %fusion.10 = f32[6,160]{1,0:T(8,128)S(1)} fusion(pred[160,1280]{1,0:T(8,128)(4,1)S(1)} %copy-done.24, bf16[160,6,64]{0,2,1:T(8,128)(2,1)} %bitcast.180, bf16[1280,6,64]{0,2,1:T(8,128)(2,1)} %bitcast.166), kind=kOutput, calls=%fused_computation.16 | convolution fusion | flops 163431680 | bytes 1314560 | tf_op jit(solution)/shard_map/sub | solution.py:284
  233.7 4.3 %fusion.36 = bf16[160,6,64]{0,2,1:T(8,128)(2,1)} fusion(bf16[1280,6,64]{0,2,1:T(8,128)(2,1)} %bitcast.172, pred[160,1280]{1,0:T(8,128)(4,1)S(1)} %copy-done.24, f32[160,6]{0,1:T(8,128)S(1)} %bitcast.187, bf16[160,6,64]{0,2,1:T(8,128)(2,1)} %bitcast.181, bf16[1280,6,64]{0,2,1:T(8,128)(2,1)} %bitcast.167), kind=kOutput, calls=%fused_computation.49 | convolution fusion | flops 320841920 | bytes 2420480 | tf_op jit(solution)/shard_map/hqk,khe->hqe/dot_general | solution.py:286
  239.1 40.0 %shard_map.230 = bf16[40,1536]{1,0:T(8,128)(2,1)S(1)} custom-call(bf16[160,384]{1,0:T(8,128)(2,1)S(1)} %copy.95.refs_0_, f32[40,1536]{1,0:T(8,128)S(1)} %get-tuple-element.15.refs_1_, f32[2,6,1536]{2,1,0:T(8,128)S(1)} %get-tuple-element.63.refs_4_.refs_2_, bf16[384,1536]{1,0:T(8,128)(2,1)S(1)} %bitcast.144, bf16[384,1536]{1,0:T(8,128)(2,1)S(1)} %bitcast.147, ...), custom_call_target="tpu_custom_call" | custom-call | tf_op jit(solution)/shard_map/pallas_call | solution.py:257
  279.3 13.7 %all_gather.23 = bf16[2,32,1536]{2,1,0:T(8,128)(2,1)S(1)} all-gather(bf16[2,8,1536]{2,1,0:T(8,128)(2,1)S(1)} %pad_maximum_fusion.12), channel_id=1, replica_groups=mesh['section'=2,'seq'=4,'tp'=4] {'tp'}, dimensions={1}, use_global_device_ids=true | all-gather | bytes 245760 | tf_op jit(solution)/shard_map/all_gather | solution.py:423
  296.9 31.4 %all-gather = f32[16,32,64]{2,1,0:T(8,128)S(1)} all-gather(f32[2,32,64]{2,1,0:T(8,128)S(1)} %fusion.90), channel_id=2, replica_groups=mesh['section'=2,'seq'=4,'tp'=4] {'section','tp'}, dimensions={0}, use_global_device_ids=true | all-gather | bytes 147456 | tf_op jit(solution)/shard_map/all_gather | solution.py:430
  (149 shorter events, 41.1 us)
Async XLA Ops:
  7.2 289.4 %copy-start = (bf16[1536,64]{0,1:T(8,128)(2,1)S(1)}, bf16[1536,64]{0,1:T(8,128)(2,1)}, u32[]{:S(2)}) copy-start(bf16[1536,64]{0,1:T(8,128)(2,1)} %param.41) | copy-start | bytes 589828
  7.2 38.5 %all-gather.3.cloned.1.call-start = ((), (), s32[]{:S(2)}) async-start(), calls=%async_computation | async-start | bytes 2457600 | tf_op jit(solution)/shard_map/all_gather | solution.py:360
  9.5 8.2 %copy-start.20 = (bf16[2,128,1536]{2,1,0:T(8,128)(2,1)S(1)}, bf16[2,128,1536]{2,1,0:T(8,128)(2,1)}, u32[]{:S(2)}) copy-start(bf16[2,128,1536]{2,1,0:T(8,128)(2,1)} %param.21) | copy-start | bytes 2359300
  11.4 12.8 %copy-start.3 = (f32[2,6,1536]{2,1,0:T(8,128)}, f32[2,6,1536]{2,1,0:T(8,128)S(1)}, u32[]{:S(2)}) copy-start(f32[2,6,1536]{2,1,0:T(8,128)S(1)} %get-tuple-element.64.refs_2_) | copy-start | bytes 221188
  17.7 6.5 %copy-start.23 = (bf16[2,32,1536]{2,1,0:T(8,128)(2,1)S(1)}, bf16[2,32,1536]{2,1,0:T(8,128)(2,1)}, u32[]{:S(2)}) copy-start(bf16[2,32,1536]{2,1,0:T(8,128)(2,1)} %param.22) | copy-start | bytes 589828
  24.6 6.1 %copy-start.31 = (s32[2,128]{1,0:T(2,128)S(1)}, s32[2,128]{1,0:T(2,128)}, u32[]{:S(2)}) copy-start(s32[2,128]{1,0:T(2,128)} %param.26) | copy-start | bytes 3076
  24.6 6.1 %copy-start.33 = (s32[2]{0:T(128)S(1)}, s32[2]{0:T(128)}, u32[]{:S(2)}) copy-start(s32[2]{0:T(128)} %param.25) | copy-start | bytes 28
  24.6 6.4 %copy-start.35 = (s32[2]{0:T(128)S(1)}, s32[2]{0:T(128)}, u32[]{:S(2)}) copy-start(s32[2]{0:T(128)} %param.24) | copy-start | bytes 28
  24.6 7.0 %copy-start.28 = (f32[2,128,64]{1,2,0:T(8,128)S(1)}, f32[2,128,64]{1,2,0:T(8,128)}, u32[]{:S(2)}) copy-start(f32[2,128,64]{1,2,0:T(8,128)} %param.23) | copy-start | bytes 196612
  28.1 16.8 %copy-start.29 = (f32[2,2,1536]{2,1,0:T(2,128)S(1)}, f32[2,2,1536]{2,1,0:T(2,128)}, u32[]{:S(2)}) copy-start(f32[2,2,1536]{2,1,0:T(2,128)} %param.32) | copy-start | bytes 73732
  29.3 19.7 %copy-start.15 = (bf16[160,768]{1,0:T(8,128)(2,1)}, bf16[160,768]{1,0:T(8,128)(2,1)S(1)}, u32[]{:S(2)}) copy-start(bf16[160,768]{1,0:T(8,128)(2,1)S(1)} %pad_maximum_fusion.6) | copy-start | bytes 737284
  33.6 19.5 %copy-start.26 = (pred[160,1280]{1,0:T(8,128)(4,1)}, pred[160,1280]{1,0:T(8,128)(4,1)S(1)}, u32[]{:S(2)}) copy-start(pred[160,1280]{1,0:T(8,128)(4,1)S(1)} %get-tuple-element.57) | copy-start | bytes 614404
  56.3 6.3 %copy-start.1 = (bf16[1,384,1536]{2,1,0:T(8,128)(2,1)S(1)}, bf16[1,384,1536]{2,1,0:T(8,128)(2,1)}, u32[]{:S(2)}) copy-start(bf16[1,384,1536]{2,1,0:T(8,128)(2,1)} %param.34) | copy-start | bytes 3538948
  56.3 6.3 %copy-start.2 = (bf16[1,384,1536]{2,1,0:T(8,128)(2,1)S(1)}, bf16[1,384,1536]{2,1,0:T(8,128)(2,1)}, u32[]{:S(2)}) copy-start(bf16[1,384,1536]{2,1,0:T(8,128)(2,1)} %param.38) | copy-start | bytes 3538948
  64.4 54.4 %copy-start.13 = (bf16[1,1536,3,384]{1,3,2,0:T(8,128)(2,1)S(1)}, bf16[1,1536,3,384]{1,3,2,0:T(8,128)(2,1)}, u32[]{:S(2)}) copy-start(bf16[1,1536,3,384]{1,3,2,0:T(8,128)(2,1)} %copy.82) | copy-start | bytes 10616836
  64.4 55.6 %copy-start.11 = (bf16[1,1536,3,384]{1,3,2,0:T(8,128)(2,1)S(1)}, bf16[1,1536,3,384]{1,3,2,0:T(8,128)(2,1)}, u32[]{:S(2)}) copy-start(bf16[1,1536,3,384]{1,3,2,0:T(8,128)(2,1)} %copy.83) | copy-start | bytes 10616836
  125.7 17.4 %copy-start.25 = (pred[160,1280]{1,0:T(8,128)(4,1)S(1)}, pred[160,1280]{1,0:T(8,128)(4,1)}, u32[]{:S(2)}) copy-start(pred[160,1280]{1,0:T(8,128)(4,1)} %get-tuple-element.58) | copy-start | bytes 614404
  125.7 17.4 %copy-start.27 = (bf16[160,384]{0,1:T(8,128)(2,1)S(1)}, bf16[160,384]{0,1:T(8,128)(2,1)}, u32[]{:S(2)}) copy-start(bf16[160,384]{0,1:T(8,128)(2,1)} %copy.88) | copy-start | bytes 368644
  152.8 56.1 %copy-start.14 = (bf16[1,1536,3,384]{1,3,2,0:T(8,128)(2,1)S(1)}, bf16[1,1536,3,384]{1,3,2,0:T(8,128)(2,1)}, u32[]{:S(2)}) copy-start(bf16[1,1536,3,384]{1,3,2,0:T(8,128)(2,1)} %copy.82) | copy-start | bytes 10616836
  152.8 57.3 %copy-start.12 = (bf16[1,1536,3,384]{1,3,2,0:T(8,128)(2,1)S(1)}, bf16[1,1536,3,384]{1,3,2,0:T(8,128)(2,1)}, u32[]{:S(2)}) copy-start(bf16[1,1536,3,384]{1,3,2,0:T(8,128)(2,1)} %copy.83) | copy-start | bytes 10616836
  213.4 16.7 %copy-start.24 = (pred[160,1280]{1,0:T(8,128)(4,1)S(1)}, pred[160,1280]{1,0:T(8,128)(4,1)}, u32[]{:S(2)}) copy-start(pred[160,1280]{1,0:T(8,128)(4,1)} %get-tuple-element.56) | copy-start | bytes 614404
  239.1 40.1 %copy-start.9 = (bf16[40,1536]{1,0:T(8,128)(2,1)S(1)}, bf16[40,1536]{1,0:T(8,128)(2,1)}, u32[]{:S(2)}) copy-start(bf16[40,1536]{1,0:T(8,128)(2,1)} %copy-done.8) | copy-start | bytes 368644
  239.1 57.5 %copy-start.30 = (f32[2,1536]{1,0:T(2,128)S(1)}, f32[2,1536]{1,0:T(2,128)}, u32[]{:S(2)}) copy-start(f32[2,1536]{1,0:T(2,128)} %get-tuple-element.77) | copy-start | bytes 36868
  239.1 89.2 %copy-start.32 = (f32[2]{0:T(128)S(1)}, f32[2]{0:T(128)}, u32[]{:S(2)}) copy-start(f32[2]{0:T(128)} %get-tuple-element.41) | copy-start | bytes 28
  (13 other events, 33.9 us)
Sparse Core Ops, SparseCore 0:
  10.5 24.5 all-gather.2

commit v3 on v2

--- a/solution.py
+++ b/solution.py
@@ -38,18 +38,21 @@
     refs = list(refs)
     take = lambda count: [refs.pop(0) for _ in range(count)]
     attended, shard, mod = take(3)
-    if not last:
+    if last:
+        earlier, other, mod_last, final = take(4)
+    else:
         following, mod_following = take(2)
     weights = take(6)
     if last:
-        (new_shard,) = take(1)
+        text_all, velocity_all = take(2)
     else:
         new_shard, next_normed, next_shard = take(3)
     held = take(6)
     part, first, send, arrive, gather, normed_i, normed_t, hidden_i, hidden_t, weight_sems = take(10)
     send_sems, recv_sems, gather_send_sems, gather_recv_sems = take(4)
-    if not last:
-        passed, passed_to, pass_sems, next_gather = take(4)
+    passed, passed_to, pass_sems, next_gather = take(4)
+    if last:
+        velocity_gather, velocity_send_sems, velocity_recv_sems = take(3)
     me = lax.axis_index("tp")
     section = lax.axis_index("section")
     loads = [
@@ -63,13 +66,12 @@
         pl.semaphore_signal(
             barrier, inc=1, device_id={"tp": peer}, device_id_type=pl.DeviceIdType.MESH
         )
-    if not last:
-        pl.semaphore_signal(
-            barrier,
-            inc=1,
-            device_id={"section": 1 - section},
-            device_id_type=pl.DeviceIdType.MESH,
-        )
+    pl.semaphore_signal(
+        barrier,
+        inc=1,
+        device_id={"section": 1 - section},
+        device_id_type=pl.DeviceIdType.MESH,
+    )
     out_i, out_t, up_i, up_t, down_i, down_t = held
     width = shard.shape[1]
     step = min(512, width)
@@ -116,23 +118,39 @@
             total = total + unpack(arrive[phase, d - 1])
         return total, copies
 
-    def gather_rows(phase, buffer):
+    def gather_start(buffer, sent, received):
         copies = []
         for d in range(1, n):
             copies.append(
                 pltpu.make_async_remote_copy(
                     src_ref=buffer.at[me],
                     dst_ref=buffer.at[me],
-                    send_sem=gather_send_sems.at[phase, d - 1],
-                    recv_sem=gather_recv_sems.at[phase, d - 1],
+                    send_sem=sent.at[d - 1],
+                    recv_sem=received.at[d - 1],
                     device_id={"tp": peers[d - 1]},
                     device_id_type=pl.DeviceIdType.MESH,
                 )
             )
             copies[-1].start()
+        return copies
+
+    def gather_rows(phase, buffer):
+        copies = gather_start(buffer, gather_send_sems.at[phase], gather_recv_sems.at[phase])
         for copy in copies:
             copy.wait_recv()
         return copies
+
+    def pass_across():
+        copy = pltpu.make_async_remote_copy(
+            src_ref=passed,
+            dst_ref=passed_to,
+            send_sem=pass_sems.at[0],
+            recv_sem=pass_sems.at[1],
+            device_id={"section": 1 - section},
+            device_id_type=pl.DeviceIdType.MESH,
+        )
+        copy.start()
+        return copy
 
     def both(values, table, function):
         return jnp.concatenate(
@@ -146,7 +164,7 @@
     loads[0].wait()
     loads[1].wait()
     product(attended[:all_images], attended[all_images:], out_i, out_t)
-    pl.semaphore_wait(barrier, n - 1 if last else n)
+    pl.semaphore_wait(barrier, n)
     total, pending = scatter_sum(0)
     first[...] = shard[...] + both(total, mod, lambda rows, table: table[2:3] * rows)
     gather[me] = pack(
@@ -179,18 +197,37 @@
     made = (first[...] + both(total, mod, lambda rows, table: table[5:6] * rows)).astype(
         jnp.bfloat16
     )
-    new_shard[...] = made
-    if not last:
+    if last:
+        rows_a = earlier[...].astype(jnp.float32)
+        rows_b = jnp.where(
+            section == 0, other[...].astype(jnp.float32), made.astype(jnp.float32)
+        )
+        next_gather[me] = jnp.concatenate(
+            [rows_a[image_rows:], rows_b[image_rows:]], axis=0
+        ).astype(jnp.bfloat16)
+        text_copies = gather_start(next_gather, gather_send_sems.at[1], gather_recv_sems.at[1])
+        normed = jnp.concatenate(
+            [
+                row_norm(rows[:image_rows], mod_last[r, 0:1], mod_last[r, 1:2])
+                for r, rows in enumerate((rows_a, rows_b))
+            ],
+            axis=0,
+        ).astype(jnp.bfloat16)
+        velocity = jnp.dot(normed, final[...], preferred_element_type=jnp.float32)
+        passed[...] = velocity
+        copy = pass_across()
+        copy.wait_recv()
+        velocity_gather[me] = jnp.where(section == 0, passed_to[...], velocity)
+        velocity_copies = gather_start(velocity_gather, velocity_send_sems, velocity_recv_sems)
+        for waiting in text_copies + velocity_copies:
+            waiting.wait_recv()
+        pending += [copy] + text_copies + velocity_copies
+        text_all[...] = next_gather[...]
+        velocity_all[...] = velocity_gather[...]
+    else:
+        new_shard[...] = made
         passed[...] = pack(made.astype(jnp.float32))
-        copy = pltpu.make_async_remote_copy(
-            src_ref=passed,
-            dst_ref=passed_to,
-            send_sem=pass_sems.at[0],
-            recv_sem=pass_sems.at[1],
-            device_id={"section": 1 - section},
-            device_id_type=pl.DeviceIdType.MESH,
-        )
-        copy.start()
+        copy = pass_across()
         copy.wait_recv()
         pending.append(copy)
         next_shard[...] = jnp.where(section == 0, following[...], unpack(passed_to[...]))
@@ -214,8 +251,8 @@
         copy.wait_send()
 
 
-def finish(n, attended, shard, mod, following, mod_following, weights):
-    last = following is None
+def finish(n, attended, shard, mod, rest, weights):
+    last = len(rest) == 4
     rows, width = attended.shape[0], shard.shape[1]
     shard_rows = shard.shape[0]
     image_rows = shard_rows * 4 // 5
@@ -224,10 +261,18 @@
     anywhere = pl.BlockSpec(memory_space=pl.ANY)
     block = (2 * shard_rows, width // 2)
     bf16, f32 = jnp.bfloat16, jnp.float32
-    operands = [attended, shard, mod] + ([] if last else [following, mod_following])
-    out_shape = [jax.ShapeDtypeStruct((shard_rows, width), bf16)]
-    if not last:
-        out_shape += [
+    operands = [attended, shard, mod] + list(rest)
+    image_total = 2 * image_rows
+    text_total = 2 * (shard_rows - image_rows)
+    if last:
+        lanes = rest[3].shape[1]
+        out_shape = [
+            jax.ShapeDtypeStruct((n, text_total, width), bf16),
+            jax.ShapeDtypeStruct((n, image_total, lanes), f32),
+        ]
+    else:
+        out_shape = [
+            jax.ShapeDtypeStruct((shard_rows, width), bf16),
             jax.ShapeDtypeStruct((rows, width), bf16),
             jax.ShapeDtypeStruct((shard_rows, width), f32),
         ]
@@ -247,7 +292,17 @@
         pltpu.SemaphoreType.DMA((6,)),
     ]
     scratch += [pltpu.SemaphoreType.DMA((2, n - 1))] * 4
-    if not last:
+    if last:
+        scratch += [
+            pltpu.VMEM((image_total, lanes), f32),
+            pltpu.VMEM((image_total, lanes), f32),
+            pltpu.SemaphoreType.DMA((2,)),
+            pltpu.VMEM((n, text_total, width), bf16),
+            pltpu.VMEM((n, image_total, lanes), f32),
+            pltpu.SemaphoreType.DMA((n - 1,)),
+            pltpu.SemaphoreType.DMA((n - 1,)),
+        ]
+    else:
         scratch += [
             pltpu.VMEM(block, bf16),
             pltpu.VMEM(block, bf16),
@@ -268,6 +323,76 @@
     )(*operands, *weights)
 
 
+def attention_kernel(request, queries, fresh, stale, query_rank, key_info, attended):
+    width = attended.shape[1]
+    rows = attended.shape[0]
+    rank, live = key_info[0, 0:1], key_info[0, 1:2]
+    newer = rank <= query_rank[...]
+    kept = jnp.broadcast_to(live > 0.0, newer.shape)
+    fresh_bias = jnp.where(newer & kept, 0.0, NEGATIVE)
+    stale_bias = jnp.where(jnp.logical_not(newer) & kept, 0.0, NEGATIVE)
+    lane = lax.broadcasted_iota(jnp.int32, (rows, 128), 1)
+    contract = (((1,), (1,)), ((), ()))
+    for first in range(0, width, 128):
+        keys = slice(first, first + 128)
+        values = slice(width + first, width + first + 128)
+        pair = queries[:, keys]
+        made = []
+        for part in range(2):
+            own = (lane >= part * HD) & (lane < (part + 1) * HD)
+            query = jnp.where(own, pair.astype(jnp.float32), 0.0).astype(jnp.bfloat16)
+            fresh_scores = lax.dot_general(
+                query, fresh[:, keys], contract, preferred_element_type=jnp.float32
+            ) * HD ** (-0.5) + fresh_bias
+            stale_scores = lax.dot_general(
+                query, stale[0, :, keys], contract, preferred_element_type=jnp.float32
+            ) * HD ** (-0.5) + stale_bias
+            rowmax = jnp.maximum(
+                jnp.max(fresh_scores, axis=-1, keepdims=True),
+                jnp.max(stale_scores, axis=-1, keepdims=True),
+            )
+            fresh_exp = jnp.exp(fresh_scores - rowmax)
+            stale_exp = jnp.exp(stale_scores - rowmax)
+            totals = jnp.sum(fresh_exp, axis=-1, keepdims=True) + jnp.sum(
+                stale_exp, axis=-1, keepdims=True
+            )
+            summed = jnp.dot(
+                fresh_exp.astype(jnp.bfloat16),
+                fresh[:, values],
+                preferred_element_type=jnp.float32,
+            ) + jnp.dot(
+                stale_exp.astype(jnp.bfloat16),
+                stale[0, :, values],
+                preferred_element_type=jnp.float32,
+            )
+            made.append(summed / totals)
+        attended[:, keys] = jnp.where(lane < HD, made[0], made[1]).astype(jnp.bfloat16)
+
+
+def attention(request, mixed, fresh, stale, query_rank, key_info):
+    rows, width = mixed.shape[0], mixed.shape[1] // 3
+    keys = fresh.shape[0]
+    whole = lambda shape: pl.BlockSpec(shape, lambda i, r: (0,) * len(shape))
+    chosen = lambda shape: pl.BlockSpec((1,) + shape, lambda i, r: (r[0], 0, 0))
+    return pl.pallas_call(
+        attention_kernel,
+        out_shape=jax.ShapeDtypeStruct((rows, width), jnp.bfloat16),
+        grid_spec=pltpu.PrefetchScalarGridSpec(
+            num_scalar_prefetch=1,
+            grid=(1,),
+            in_specs=[
+                whole((rows, width)),
+                whole((keys, 2 * width)),
+                chosen((keys, 2 * width)),
+                whole((rows, 1)),
+                chosen((2, keys)),
+            ],
+            out_specs=whole((rows, width)),
+        ),
+        compiler_params=pltpu.CompilerParams(vmem_limit_bytes=40 * 1024 * 1024),
+    )(request[None], mixed, fresh, stale, query_rank, key_info)
+
+
 def sigma_of(index_value):
     progress = 1.0 - index_value / STEPS
     return TIME_SHIFT * progress / (1.0 + (TIME_SHIFT - 1.0) * progress)
@@ -293,27 +418,33 @@
     return jnp.transpose(result, (1, 0, 2)).reshape(queries.shape).astype(jnp.bfloat16)
 
 
-def allowed_keys(patch_order, live, image_local, text_local, seq_count):
+def ranks_of(patch_order, image_local, text_local):
     slot_count = patch_order.shape[0]
     order = jnp.arange(slot_count, dtype=jnp.int32)
     rank = jnp.sum(
         jnp.where(patch_order[:, None] == order[None, :], order[:, None], 0), axis=0
     )
-    local = jnp.concatenate(
+    return jnp.concatenate(
         [
             jnp.repeat(rank, image_local // slot_count),
             jnp.repeat(order, text_local // slot_count),
         ]
     )
-    keys = jnp.tile(local, seq_count)
-    fresh = keys[None, :] <= local[:, None]
-    kept = jnp.concatenate(
+
+
+def kept_keys(live, image_local, text_local, seq_count):
+    return jnp.concatenate(
         [
             jnp.ones((live.shape[0], seq_count, image_local), jnp.bool_),
             live.reshape(live.shape[0], seq_count, text_local),
         ],
         axis=2,
-    ).reshape(live.shape[0], 1, -1)
+    ).reshape(live.shape[0], -1)
+
+
+def allowed_keys(local, kept, seq_count):
+    fresh = jnp.tile(local, seq_count)[None, :] <= local[:, None]
+    kept = kept[:, None, :]
     return jnp.concatenate([fresh[None] & kept, ~fresh[None] & kept], axis=2)
 
 
@@ -349,7 +480,8 @@
     text_total = text_keep.shape[1]
     positions = jnp.arange(text_total, dtype=jnp.int32)
     live = (positions[None, :] < text_length[:, None]) & (text_keep == 1)
-    allowed = allowed_keys(patch_order, live, image_local, text_local, seq_count)
+    local_rank = ranks_of(patch_order, image_local, text_local)
+    kept = kept_keys(live, image_local, text_local, seq_count)
     stale_local = jnp.concatenate(
         [
             stale_image_kv[0].reshape(requests, image_local, 2 * local_width),
@@ -363,6 +495,8 @@
         image_local == 4 * text_local
         and text_local % (8 * tp_size) == 0
         and local_width % 128 == 0
+        and requests == 2
+        and latent.shape[2] <= 128
     )
     if shapes_fit:
         tp_count = lax.axis_size("tp")
@@ -396,40 +530,52 @@
             ],
             axis=0,
         ).astype(jnp.bfloat16)
+        query_rank = local_rank.astype(jnp.float32)[:, None]
+        key_rank = jnp.tile(local_rank, seq_count).astype(jnp.float32)
+        key_info = jnp.stack(
+            [jnp.broadcast_to(key_rank, kept.shape), kept.astype(jnp.float32)], axis=1
+        )
+        lanes = 128
+        final_lanes = jnp.pad(
+            final_weight, ((0, 0), (0, lanes - final_weight.shape[1]))
+        )
         made_rows, made_kv = [], []
         for moment in range(requests + 1):
-            pick = picker(moment)
+            request = jnp.clip(moment - section_index, 0, requests - 1)
             mixed = jnp.concatenate(
                 [dot(normed[:image_local], qkv_i), dot(normed[image_local:], qkv_t)], axis=0
             ).astype(jnp.bfloat16)
-            queries, fresh_local = mixed[:, :local_width], mixed[:, local_width:]
+            fresh_local = mixed[:, local_width:]
             fresh = lax.all_gather(fresh_local, "seq", axis=0, tiled=True)
-            both = jnp.concatenate([fresh, pick(stale)], axis=0)
-            attended = attend(queries, both[:, :local_width], both[:, local_width:], pick(allowed))
+            attended = attention(request, mixed, fresh, stale, query_rank, key_info)
             made_kv.append(fresh_local)
             if moment < requests:
                 following = picker(moment + 1)
                 new_rows, normed, next_shard = finish(
-                    tp_count, attended, shard, mod, following(shards), following(mods), weights
+                    tp_count, attended, shard, mod, (following(shards), following(mods)), weights
                 )
                 shard, mod = next_shard, following(mods)
+                made_rows.append(new_rows)
             else:
-                (new_rows,) = finish(tp_count, attended, shard, mod, None, None, weights)
-            made_rows.append(new_rows)
-        choose = lambda made: jnp.stack(
-            [jnp.where(first_section, made[r], made[r + 1]) for r in range(requests)]
-        )
-        shard_out, kv_out = choose(made_rows), choose(made_kv)
-        text_out = lax.all_gather(shard_out[:, image_shard:], "tp", axis=1, tiled=True)
-        final_normed = row_norm(
-            shard_out[:, :image_shard].astype(jnp.float32), mod_final[:, :1], mod_final[:, 1:]
-        ).astype(jnp.bfloat16)
-        velocity = dot(final_normed.reshape(-1, model_width), final_weight).reshape(
-            requests, image_shard, -1
-        )
-        gathered = lax.all_gather(velocity, ("section", "tp"), axis=0)
-        velocity_used = jnp.concatenate(list(gathered[tp_count:]), axis=1)
+                earlier = jnp.where(first_section, made_rows[0], made_rows[1])
+                text_all, velocity_all = finish(
+                    tp_count,
+                    attended,
+                    shard,
+                    mod,
+                    (earlier, made_rows[1], mod_final, final_lanes),
+                    weights,
+                )
+        kv_out = jnp.stack(
+            [jnp.where(first_section, made_kv[r], made_kv[r + 1]) for r in range(requests)]
+        )
+        regroup = lambda values, rows: jnp.swapaxes(
+            values.reshape(tp_count, requests, rows, -1), 0, 1
+        ).reshape(requests, tp_count * rows, -1)
+        text_out = regroup(text_all, text_shard)
+        velocity_used = regroup(velocity_all, image_shard)[:, :, : latent.shape[2]]
     else:
+        allowed = allowed_keys(local_rank, kept, seq_count)
         qkv_i = qkv_image[0].reshape(model_width, -1)
         qkv_t = qkv_text[0].reshape(model_width, -1)
         inputs = jnp.concatenate([hidden_image, hidden_text], axis=1)

time: 339 us -> 257 us (0.76)
  blocking collectives: 74.6 us -> 29.9 us
  local copies, waits for them, and re-layouts: 49 us -> 24.5 us
  matrix products: 32.8 us -> 9.38 us
  Pallas kernels: 150 us -> 169 us
  other arithmetic: 16 us -> 8.84 us
    all_gather x2 -> x0, blocking collectives: 45 us -> none  [the longest x1 31.4 us: on_device(): gathered = lax.all_gather(velocity, ('section', 'tp'), axis=0)]
    slice x9 -> x0, local copies, waits for them, and re-layouts: 15.4 us -> none  [the longest x3 6.12 us: on_device(): both[:, :local_width]]
    dot_general x3 -> x0, matrix products: 13.2 us -> none  [attend(): jnp.einsum('hqk,khe->hqe', exponent.astype(jnp.bfloat16), split(values),...]
    sub x3 -> x0, matrix products: 10.1 us -> none  [attend(): exponent = jnp.where(allowed[None], jnp.exp(scores - rowmax), 0.0)]
    pallas_call x3, Pallas kernels: 150 us -> 160 us  [finish(): pl.pallas_call(functools.partial(finish_kernel, n, image_rows, shard_rows...]
    pallas_call x0 -> x3, Pallas kernels: none -> 9.11 us  [attention(): pl.pallas_call(attention_kernel, out_shape=jax.ShapeDtypeStruct((rows, wi...]
    concatenate x3 -> x1, other arithmetic: 6.45 us -> 0.01 us  [ranks_of(): jnp.concatenate([jnp.repeat(rank, image_local // slot_count), jnp.repeat(...]
    convert_element_type x3 -> x2, local copies, waits for them, and re-layouts: 3.79 us -> 0.17 us  [the longest x1 0.09 us: on_device(): kept.astype(jnp.float32)]
  transfers between devices with their start and end apart: 1 -> 1, of which waited for: 0 -> 0; matrix products, arithmetic and copies ran while one was open for 7% -> 11% of each run, Pallas kernels for 0% -> 0%
where the time goes in v3:
time: 257 us; the launch traced here: 256 us
  Pallas kernels  169 us (66%)
  blocking collectives  29.9 us (12%)
  local copies, waits for them, and re-layouts  24.5 us (10%)
  between operations  14.6 us (6%)
  matrix products  9.38 us (4%)
  other arithmetic  8.84 us (3%)
    pallas_call x3, Pallas kernels, finish(): pl.pallas_call(functools.partial(finish_kernel, n, image_rows, shard_rows...  160 us
    all_gather x3, blocking collectives, on_device(): fresh = lax.all_gather(fresh_local, 'seq', axis=0, tiled=True)  29.9 us
    unnamed x57, local copies, waits for them, and re-layouts  17.5 us
    dot_general x6, matrix products, on_device(): jnp.dot(left, right, preferred_element_type=jnp.float32)  9.38 us
    pallas_call x3, Pallas kernels, attention(): pl.pallas_call(attention_kernel, out_shape=jax.ShapeDtypeStruct((rows, wi...  9.11 us
  transfers between devices with their start and end apart: 1, of which 0 were waited for; matrix products, arithmetic and copies ran while one was open for 11% of the time, Pallas kernels for 0%

profile of v3, /device:TPU:0, one launch (start us, length us, event | category | flops | bytes accessed | tf_op | source)
XLA Modules:
  0.0 256.4 jit_solution(10040160621594314266)
XLA Ops:
  7.2 1.0 reshape_squeeze.15
  8.2 1.2 reshape_squeeze.14
  11.3 1.0 convert_reduce_fusion.1
  12.3 1.1 fusion.22
  13.5 1.1 convert_reduce_fusion
  14.6 1.2 fusion.3
  18.6 6.1 %copy.58 = bf16[1,1536,3,384]{1,3,2,0:T(8,128)(2,1)} copy(bf16[1,1536,3,384]{3,1,2,0:T(8,128)(2,1)} %param.37) | data formatting | bytes 7077888 | tf_op args[16]
  24.8 6.1 %copy.57 = bf16[1,1536,3,384]{1,3,2,0:T(8,128)(2,1)} copy(bf16[1,1536,3,384]{3,1,2,0:T(8,128)(2,1)} %param.33) | data formatting | bytes 7077888 | tf_op args[12]
  32.2 3.5 %convolution_convert_fusion.5 = bf16[32,1152]{1,0:T(8,128)(2,1)S(1)} fusion(bf16[1536,1152]{0,1:T(8,128)(2,1)} %bitcast.91, f32[1536]{0:T(1024)S(1)} %get-tuple-element.33, f32[1536]{0:T(1024)S(1)} %get-tuple-element.34, f32[32]{0:T(128)S(1)} %add_rsqrt_fusion, f32[32]{0:T(128)S(1)} %broadcast_multiply_fusion, bf16[2,32,1536]{2,1,0:T(8,128)(2,1)S(1)} %copy-done.19), kind=kOutput, calls=%fused_computation.5 | convolution fusion | flops 113577984 | bytes 3728384 | tf_op jit(solution)/shard_map/dot_general | solution.py:518
  35.7 1.3 convolution_convert_fusion.2
  37.9 11.3 %all_gather.12.fresh = bf16[640,768]{1,0:T(8,128)(2,1)S(1)} all-gather(bf16[160,768]{1,0:T(8,128)(2,1)S(1)} %fusion.18), channel_id=1, replica_groups=mesh['section'=2,'seq'=4,'tp'=4] {'seq'}, dimensions={0}, use_global_device_ids=true | all-gather | bytes 1228800 | tf_op jit(solution)/shard_map/all_gather | solution.py:549
  50.1 1.5 copy-done
  52.7 3.0 %shard_map.228.refs_0_ = bf16[160,384]{1,0:T(8,128)(2,1)S(1)} custom-call(s32[1]{0:T(128)} %bitcast.2.request, bf16[160,1152]{1,0:T(8,128)(2,1)S(1)} %copy-done.5, bf16[640,768]{1,0:T(8,128)(2,1)S(1)} %all_gather.12.fresh, bf16[2,640,768]{2,1,0:T(8,128)(2,1)S(1)} %copy-done, f32[160,1]{1,0:T(8,128)S(1)} %convert_element_type.59.query_rank, ...), custom_call_target="tpu_custom_call" | custom-call | tf_op jit(solution)/shard_map/pallas_call | solution.py:377
  55.8 54.4 %shard_map.229 = (bf16[40,1536]{1,0:T(8,128)(2,1)S(1)}, bf16[160,1536]{1,0:T(8,128)(2,1)S(1)}, f32[40,1536]{1,0:T(8,128)S(1)}) custom-call(bf16[160,384]{1,0:T(8,128)(2,1)S(1)} %shard_map.228.refs_0_, f32[40,1536]{1,0:T(8,128)S(1)} %copy-done.8, f32[2,6,1536]{2,1,0:T(8,128)S(1)} %copy-done.11, f32[40,1536]{1,0:T(8,128)S(1)} %copy-done.7, ...), custom_call_target="tpu_custom_call" | custom-call | tf_op jit(solution)/shard_map/pallas_call | solution.py:312
  110.1 1.1 convolution_convert_fusion.4
  112.1 1.2 convolution_convert_fusion.1
  113.5 9.5 %all_gather.14.fresh = bf16[640,768]{1,0:T(8,128)(2,1)S(1)} all-gather(bf16[160,768]{1,0:T(8,128)(2,1)S(1)} %get-tuple-element.39), channel_id=1, replica_groups=mesh['section'=2,'seq'=4,'tp'=4] {'seq'}, dimensions={0}, use_global_device_ids=true | all-gather | bytes 1228800 | tf_op jit(solution)/shard_map/all_gather | solution.py:549
  123.0 3.0 %shard_map.230.refs_0_ = bf16[160,384]{1,0:T(8,128)(2,1)S(1)} custom-call(s32[1]{0:T(128)} %bitcast.1.request, bf16[160,1152]{1,0:T(8,128)(2,1)S(1)} %pad_maximum_fusion.2.queries, bf16[640,768]{1,0:T(8,128)(2,1)S(1)} %all_gather.14.fresh, bf16[2,640,768]{2,1,0:T(8,128)(2,1)S(1)} %copy-done.1, f32[160,1]{1,0:T(8,128)S(1)} %convert_element_type.59.query_rank, ...), custom_call_target="tpu_custom_call" | custom-call | tf_op jit(solution)/shard_map/pallas_call | solution.py:377
  126.0 55.2 %shard_map.231 = (bf16[40,1536]{1,0:T(8,128)(2,1)S(1)}, bf16[160,1536]{1,0:T(8,128)(2,1)S(1)}, f32[40,1536]{1,0:T(8,128)S(1)}) custom-call(bf16[160,384]{1,0:T(8,128)(2,1)S(1)} %shard_map.230.refs_0_, f32[40,1536]{1,0:T(8,128)S(1)} %get-tuple-element.13.refs_1_, f32[2,6,1536]{2,1,0:T(8,128)S(1)} %copy-done.9, f32[40,1536]{1,0:T(8,128)S(1)} %copy-done.6, ...), custom_call_target="tpu_custom_call" | custom-call | tf_op jit(solution)/shard_map/pallas_call | solution.py:312
  181.2 1.1 convolution_convert_fusion.3
  182.3 1.3 convolution_convert_fusion
  183.8 9.1 %all_gather.15.fresh = bf16[640,768]{1,0:T(8,128)(2,1)S(1)} all-gather(bf16[160,768]{1,0:T(8,128)(2,1)S(1)} %get-tuple-element.37), channel_id=1, replica_groups=mesh['section'=2,'seq'=4,'tp'=4] {'seq'}, dimensions={0}, use_global_device_ids=true | all-gather | bytes 1228800 | tf_op jit(solution)/shard_map/all_gather | solution.py:549
  192.9 3.0 %shard_map.232.refs_0_ = bf16[160,384]{1,0:T(8,128)(2,1)S(1)} custom-call(s32[1]{0:T(128)} %bitcast.request, bf16[160,1152]{1,0:T(8,128)(2,1)S(1)} %pad_maximum_fusion.3.queries, bf16[640,768]{1,0:T(8,128)(2,1)S(1)} %all_gather.15.fresh, bf16[2,640,768]{2,1,0:T(8,128)(2,1)S(1)} %copy-done.1, f32[160,1]{1,0:T(8,128)S(1)} %convert_element_type.59.query_rank, ...), custom_call_target="tpu_custom_call" | custom-call | tf_op jit(solution)/shard_map/pallas_call | solution.py:377
  196.0 50.5 %shard_map.233 = (bf16[4,16,1536]{2,1,0:T(8,128)(2,1)S(1)}, f32[4,64,128]{2,1,0:T(8,128)S(1)}) custom-call(bf16[160,384]{1,0:T(8,128)(2,1)S(1)} %shard_map.232.refs_0_, f32[40,1536]{1,0:T(8,128)S(1)} %get-tuple-element.15.refs_1_, f32[2,6,1536]{2,1,0:T(8,128)S(1)} %get-tuple-element.45.refs_4_.refs_2_, bf16[40,1536]{1,0:T(8,128)(2,1)S(1)} %broadcast_select_fusion.refs_3_, ...), custom_call_target="tpu_custom_call" | custom-call | tf_op jit(solution)/shard_map/pallas_call | solution.py:312
  (105 shorter events, 12.9 us)
Async XLA Ops:
  7.2 9.9 %copy-start.22 = (f32[1,2,6,1536]{3,1,2,0:T(2,128)S(1)}, f32[1,2,6,1536]{3,1,2,0:T(2,128)}, u32[]{:S(2)}) copy-start(f32[1,2,6,1536]{3,1,2,0:T(2,128)} %param.31) | copy-start | bytes 221188
  7.2 9.9 %copy-start.23 = (f32[1,2,6,1536]{3,1,2,0:T(2,128)S(1)}, f32[1,2,6,1536]{3,1,2,0:T(2,128)}, u32[]{:S(2)}) copy-start(f32[1,2,6,1536]{3,1,2,0:T(2,128)} %param.30) | copy-start | bytes 221188
  7.2 10.7 %copy-start.24 = (f32[2,128,64]{1,2,0:T(8,128)S(1)}, f32[2,128,64]{1,2,0:T(8,128)}, u32[]{:S(2)}) copy-start(f32[2,128,64]{1,2,0:T(8,128)} %param.23) | copy-start | bytes 196612
  7.2 42.9 %all-gather.2.cloned.1.call-start = ((), (), s32[]{:S(2)}) async-start(), calls=%async_computation | async-start | bytes 2457600 | tf_op jit(solution)/shard_map/all_gather | solution.py:492
  17.9 14.2 %copy-start.10 = (f32[2,6,1536]{2,1,0:T(8,128)}, f32[2,6,1536]{2,1,0:T(8,128)S(1)}, u32[]{:S(2)}) copy-start(f32[2,6,1536]{2,1,0:T(8,128)S(1)} %get-tuple-element.46.refs_2_) | copy-start | bytes 221188
  24.8 6.2 %copy-start.21 = (bf16[1536,64]{0,1:T(8,128)(2,1)S(1)}, bf16[1536,64]{0,1:T(8,128)(2,1)}, u32[]{:S(2)}) copy-start(bf16[1536,64]{0,1:T(8,128)(2,1)} %param.41) | copy-start | bytes 589828
  24.8 7.4 %copy-start.19 = (bf16[2,32,1536]{2,1,0:T(8,128)(2,1)S(1)}, bf16[2,32,1536]{2,1,0:T(8,128)(2,1)}, u32[]{:S(2)}) copy-start(bf16[2,32,1536]{2,1,0:T(8,128)(2,1)} %param.22) | copy-start | bytes 589828
  30.9 4.8 %copy-start.18 = (bf16[2,128,1536]{2,1,0:T(8,128)(2,1)S(1)}, bf16[2,128,1536]{2,1,0:T(8,128)(2,1)}, u32[]{:S(2)}) copy-start(bf16[2,128,1536]{2,1,0:T(8,128)(2,1)} %param.21) | copy-start | bytes 2359300
  31.2 4.4 %copy-start.14 = (bf16[1,1536,3,384]{1,3,2,0:T(8,128)(2,1)S(1)}, bf16[1,1536,3,384]{1,3,2,0:T(8,128)(2,1)}, u32[]{:S(2)}) copy-start(bf16[1,1536,3,384]{1,3,2,0:T(8,128)(2,1)} %copy.57) | copy-start | bytes 10616836
  32.1 4.8 %copy-start.25 = (s32[2]{0:T(128)S(1)}, s32[2]{0:T(128)}, u32[]{:S(2)}) copy-start(s32[2]{0:T(128)} %param.24) | copy-start | bytes 28
  37.8 17.8 %copy-start.2 = (bf16[1,384,1536]{2,1,0:T(8,128)(2,1)S(1)}, bf16[1,384,1536]{2,1,0:T(8,128)(2,1)}, u32[]{:S(2)}) copy-start(bf16[1,384,1536]{2,1,0:T(8,128)(2,1)} %param.34) | copy-start | bytes 3538948
  37.8 17.9 %copy-start.3 = (bf16[1,384,1536]{2,1,0:T(8,128)(2,1)S(1)}, bf16[1,384,1536]{2,1,0:T(8,128)(2,1)}, u32[]{:S(2)}) copy-start(bf16[1,384,1536]{2,1,0:T(8,128)(2,1)} %param.38) | copy-start | bytes 3538948
  52.6 3.1 %copy-start.7 = (f32[40,1536]{1,0:T(8,128)S(1)}, f32[40,1536]{1,0:T(8,128)}, u32[]{:S(2)}) copy-start(f32[40,1536]{1,0:T(8,128)} %get-tuple-element.43.refs_3_) | copy-start | bytes 737284
  52.7 3.1 %copy-start.8 = (f32[40,1536]{1,0:T(8,128)S(1)}, f32[40,1536]{1,0:T(8,128)}, u32[]{:S(2)}) copy-start(f32[40,1536]{1,0:T(8,128)} %get-tuple-element.44.refs_1_) | copy-start | bytes 737284
  52.7 3.1 %copy-start.9 = (f32[2,6,1536]{2,1,0:T(8,128)S(1)}, f32[2,6,1536]{2,1,0:T(8,128)}, u32[]{:S(2)}) copy-start(f32[2,6,1536]{2,1,0:T(8,128)} %get-tuple-element.47.refs_4_.refs_2_) | copy-start | bytes 221188
  52.7 3.1 %copy-start.11 = (f32[2,6,1536]{2,1,0:T(8,128)S(1)}, f32[2,6,1536]{2,1,0:T(8,128)}, u32[]{:S(2)}) copy-start(f32[2,6,1536]{2,1,0:T(8,128)} %copy-done.10) | copy-start | bytes 221188
  55.7 54.4 %copy-start.13 = (bf16[1,1536,3,384]{1,3,2,0:T(8,128)(2,1)S(1)}, bf16[1,1536,3,384]{1,3,2,0:T(8,128)(2,1)}, u32[]{:S(2)}) copy-start(bf16[1,1536,3,384]{1,3,2,0:T(8,128)(2,1)} %copy.58) | copy-start | bytes 10616836
  110.1 2.0 copy-start.15
  110.1 3.3 %copy-start.17 = (bf16[160,768]{1,0:T(8,128)(2,1)S(1)}, bf16[160,768]{1,0:T(8,128)(2,1)}, u32[]{:S(2)}) copy-start(bf16[160,768]{1,0:T(8,128)(2,1)} %copy-done.16) | copy-start | bytes 737284
  112.1 10.9 %copy-start.1 = (bf16[2,640,768]{2,1,0:T(8,128)(2,1)S(1)}, bf16[2,640,768]{2,1,0:T(8,128)(2,1)}, u32[]{:S(2)}) copy-start(bf16[2,640,768]{2,1,0:T(8,128)(2,1)} %all-gather.2.cloned.1.call-done.stale) | copy-start | bytes 5898244
  113.3 12.7 %copy-start.6 = (f32[40,1536]{1,0:T(8,128)S(1)}, f32[40,1536]{1,0:T(8,128)}, u32[]{:S(2)}) copy-start(f32[40,1536]{1,0:T(8,128)} %get-tuple-element.42.refs_3_) | copy-start | bytes 737284
  183.7 12.2 %copy-start.4 = (bf16[1536,128]{1,0:T(8,128)(2,1)S(1)}, bf16[1536,128]{1,0:T(8,128)(2,1)}, u32[]{:S(2)}) copy-start(bf16[1536,128]{1,0:T(8,128)(2,1)} %pad.5.refs_6_) | copy-start | bytes 1179652
  183.7 12.2 %copy-start.12 = (f32[2,2,1536]{2,1,0:T(2,128)S(1)}, f32[2,2,1536]{2,1,0:T(2,128)}, u32[]{:S(2)}) copy-start(f32[2,2,1536]{2,1,0:T(2,128)} %refs_5_.1) | copy-start | bytes 73732
  195.9 50.6 %copy-start.20 = (f32[2,128,64]{2,1,0:T(8,128)S(1)}, f32[2,128,64]{2,1,0:T(8,128)}, u32[]{:S(2)}) copy-start(f32[2,128,64]{2,1,0:T(8,128)} %copy.62) | copy-start | bytes 196612
  (3 other events, 3.4 us)
Sparse Core Ops, SparseCore 0:
  10.5 24.6 all-gather.1

commit v4 on v3

--- a/solution.py
+++ b/solution.py
@@ -323,29 +323,89 @@
     )(*operands, *weights)
 
 
-def attention_kernel(request, queries, fresh, stale, query_rank, key_info, attended):
-    width = attended.shape[1]
-    rows = attended.shape[0]
-    rank, live = key_info[0, 0:1], key_info[0, 1:2]
+def front_kernel(moment, all_images, *refs):
+    normed, weight_i, weight_t, stale, query_rank, key_info = refs[:6]
+    attended, own_kv = refs[6:8]
+    held_i, held_t, queries, fresh, weight_sems, send_sems, recv_sems = refs[8:]
+    rows, width = attended.shape
+    me = lax.axis_index("seq")
+    count = fresh.shape[0]
+    sibling = me + 1 - 2 * lax.rem(me, 2)
+    across = lax.rem(me + 2, count)
+    request = jnp.clip(moment - lax.axis_index("section"), 0, stale.shape[0] - 1)
+    order = (1, 2, 0)
+    loads = []
+    for j in order:
+        for stream, (weight, held) in enumerate(((weight_i, held_i), (weight_t, held_t))):
+            loads.append(
+                pltpu.make_async_copy(weight.at[j], held.at[j], weight_sems.at[stream, j])
+            )
+            loads[-1].start()
+    barrier = pltpu.get_barrier_semaphore()
+    for peer in (sibling, across):
+        pl.semaphore_signal(
+            barrier, inc=1, device_id={"seq": peer}, device_id_type=pl.DeviceIdType.MESH
+        )
+
+    def projected(index):
+        loads[2 * index].wait()
+        loads[2 * index + 1].wait()
+        j = order[index]
+        return jnp.concatenate(
+            [
+                jnp.dot(normed[:all_images], held_i[j], preferred_element_type=jnp.float32),
+                jnp.dot(normed[all_images:], held_t[j], preferred_element_type=jnp.float32),
+            ],
+            axis=0,
+        ).astype(jnp.bfloat16)
+
+    def sending(slot, peer, index):
+        return pltpu.make_async_remote_copy(
+            src_ref=fresh.at[slot],
+            dst_ref=fresh.at[slot],
+            send_sem=send_sems.at[index],
+            recv_sem=recv_sems.at[index],
+            device_id={"seq": peer},
+            device_id_type=pl.DeviceIdType.MESH,
+        )
+
+    for part in range(2):
+        block = projected(part)
+        own_kv[:, part * width : (part + 1) * width] = block
+        fresh[me, :, part * width : (part + 1) * width] = block
+    pl.semaphore_wait(barrier, 2)
+    over_y = sending(me, across, 0)
+    over_y.start()
+    over_core = sending(me, sibling, 1)
+    over_core.start()
+    queries[...] = projected(2)
+    rank, live = key_info[request, 0:1], key_info[request, 1:2]
     newer = rank <= query_rank[...]
     kept = jnp.broadcast_to(live > 0.0, newer.shape)
     fresh_bias = jnp.where(newer & kept, 0.0, NEGATIVE)
     stale_bias = jnp.where(jnp.logical_not(newer) & kept, 0.0, NEGATIVE)
+    over_y.wait_recv()
+    forward = sending(across, sibling, 2)
+    forward.start()
+    over_core.wait_recv()
+    forward.wait_recv()
     lane = lax.broadcasted_iota(jnp.int32, (rows, 128), 1)
     contract = (((1,), (1,)), ((), ()))
     for first in range(0, width, 128):
         keys = slice(first, first + 128)
         values = slice(width + first, width + first + 128)
         pair = queries[:, keys]
+        fresh_keys = fresh[:, :, keys].reshape(-1, 128)
+        fresh_values = fresh[:, :, values].reshape(-1, 128)
         made = []
         for part in range(2):
             own = (lane >= part * HD) & (lane < (part + 1) * HD)
             query = jnp.where(own, pair.astype(jnp.float32), 0.0).astype(jnp.bfloat16)
             fresh_scores = lax.dot_general(
-                query, fresh[:, keys], contract, preferred_element_type=jnp.float32
+                query, fresh_keys, contract, preferred_element_type=jnp.float32
             ) * HD ** (-0.5) + fresh_bias
             stale_scores = lax.dot_general(
-                query, stale[0, :, keys], contract, preferred_element_type=jnp.float32
+                query, stale[request, :, keys], contract, preferred_element_type=jnp.float32
             ) * HD ** (-0.5) + stale_bias
             rowmax = jnp.maximum(
                 jnp.max(fresh_scores, axis=-1, keepdims=True),
@@ -358,39 +418,47 @@
             )
             summed = jnp.dot(
                 fresh_exp.astype(jnp.bfloat16),
-                fresh[:, values],
+                fresh_values,
                 preferred_element_type=jnp.float32,
             ) + jnp.dot(
                 stale_exp.astype(jnp.bfloat16),
-                stale[0, :, values],
+                stale[request, :, values],
                 preferred_element_type=jnp.float32,
             )
             made.append(summed / totals)
         attended[:, keys] = jnp.where(lane < HD, made[0], made[1]).astype(jnp.bfloat16)
-
-
-def attention(request, mixed, fresh, stale, query_rank, key_info):
-    rows, width = mixed.shape[0], mixed.shape[1] // 3
-    keys = fresh.shape[0]
-    whole = lambda shape: pl.BlockSpec(shape, lambda i, r: (0,) * len(shape))
-    chosen = lambda shape: pl.BlockSpec((1,) + shape, lambda i, r: (r[0], 0, 0))
+    for copy in (over_y, over_core, forward):
+        copy.wait_send()
+
+
+def front(moment, seq_count, all_images, normed, weight_i, weight_t, stale, query_rank, key_info):
+    rows, width = normed.shape[0], weight_i.shape[2]
+    vmem = pl.BlockSpec(memory_space=pltpu.VMEM)
+    anywhere = pl.BlockSpec(memory_space=pl.ANY)
+    bf16 = jnp.bfloat16
     return pl.pallas_call(
-        attention_kernel,
-        out_shape=jax.ShapeDtypeStruct((rows, width), jnp.bfloat16),
-        grid_spec=pltpu.PrefetchScalarGridSpec(
-            num_scalar_prefetch=1,
-            grid=(1,),
-            in_specs=[
-                whole((rows, width)),
-                whole((keys, 2 * width)),
-                chosen((keys, 2 * width)),
-                whole((rows, 1)),
-                chosen((2, keys)),
-            ],
-            out_specs=whole((rows, width)),
+        functools.partial(front_kernel, moment, all_images),
+        out_shape=[
+            jax.ShapeDtypeStruct((rows, width), bf16),
+            jax.ShapeDtypeStruct((rows, 2 * width), bf16),
+        ],
+        in_specs=[vmem, anywhere, anywhere, vmem, vmem, vmem],
+        out_specs=[vmem, vmem],
+        scratch_shapes=[
+            pltpu.VMEM(weight_i.shape, bf16),
+            pltpu.VMEM(weight_t.shape, bf16),
+            pltpu.VMEM((rows, width), bf16),
+            pltpu.VMEM((seq_count, rows, 2 * width), bf16),
+            pltpu.SemaphoreType.DMA((2, 3)),
+            pltpu.SemaphoreType.DMA((3,)),
+            pltpu.SemaphoreType.DMA((3,)),
+        ],
+        compiler_params=pltpu.CompilerParams(
+            collective_id=2 + moment,
+            has_side_effects=True,
+            vmem_limit_bytes=40 * 1024 * 1024,
         ),
-        compiler_params=pltpu.CompilerParams(vmem_limit_bytes=40 * 1024 * 1024),
-    )(request[None], mixed, fresh, stale, query_rank, key_info)
+    )(normed, weight_i, weight_t, stale, query_rank, key_info)
 
 
 def sigma_of(index_value):
@@ -496,12 +564,13 @@
         and text_local % (8 * tp_size) == 0
         and local_width % 128 == 0
         and requests == 2
+        and seq_count == 4
         and latent.shape[2] <= 128
     )
     if shapes_fit:
         tp_count = lax.axis_size("tp")
-        qkv_i = qkv_image[0].reshape(model_width, -1)
-        qkv_t = qkv_text[0].reshape(model_width, -1)
+        qkv_i = jnp.swapaxes(qkv_image[0], 0, 1)
+        qkv_t = jnp.swapaxes(qkv_text[0], 0, 1)
         tp_index = lax.axis_index("tp")
         image_shard, text_shard = image_local // tp_count, text_local // tp_count
         shards = jnp.concatenate(
@@ -541,13 +610,9 @@
         )
         made_rows, made_kv = [], []
         for moment in range(requests + 1):
-            request = jnp.clip(moment - section_index, 0, requests - 1)
-            mixed = jnp.concatenate(
-                [dot(normed[:image_local], qkv_i), dot(normed[image_local:], qkv_t)], axis=0
-            ).astype(jnp.bfloat16)
-            fresh_local = mixed[:, local_width:]
-            fresh = lax.all_gather(fresh_local, "seq", axis=0, tiled=True)
-            attended = attention(request, mixed, fresh, stale, query_rank, key_info)
+            attended, fresh_local = front(
+                moment, seq_count, image_local, normed, qkv_i, qkv_t, stale, query_rank, key_info
+            )
             made_kv.append(fresh_local)
             if moment < requests:
                 following = picker(moment + 1)

time: 257 us -> 265 us (1.031)
  Pallas kernels: 169 us -> 206 us
  blocking collectives: 29.9 us -> 0 us
  matrix products: 9.38 us -> 0 us
  other arithmetic: 8.84 us -> 16.8 us
    pallas_call x3, Pallas kernels: 9.11 us -> 39.5 us  [front(): pl.pallas_call(functools.partial(front_kernel, moment, all_images), out_s...]
    all_gather x3 -> x0, blocking collectives: 29.9 us -> none  [on_device(): fresh = lax.all_gather(fresh_local, 'seq', axis=0, tiled=True)]
    dot_general x6 -> x0, matrix products: 9.38 us -> none  [on_device(): jnp.dot(left, right, preferred_element_type=jnp.float32)]
    pallas_call x3, Pallas kernels: 160 us -> 166 us  [finish(): pl.pallas_call(functools.partial(finish_kernel, n, image_rows, shard_rows...]
    unnamed x57 -> x71, local copies, waits for them, and re-layouts: 17.5 us -> 13.1 us
  transfers between devices with their start and end apart: 1 -> 1, of which waited for: 0 -> 0; matrix products, arithmetic and copies ran while one was open for 11% -> 10% of each run, Pallas kernels for 0% -> 0%
where the time goes in v4:
time: 265 us; the launch traced here: 264 us
  Pallas kernels  206 us (78%)
  local copies, waits for them, and re-layouts  27.1 us (10%)
  other arithmetic  16.8 us (6%)
  between operations  14.5 us (5%)
    pallas_call x3, Pallas kernels, finish(): pl.pallas_call(functools.partial(finish_kernel, n, image_rows, shard_rows...  166 us
    pallas_call x3, Pallas kernels, front(): pl.pallas_call(functools.partial(front_kernel, moment, all_images), out_s...  39.5 us
    unnamed x71, local copies, waits for them, and re-layouts  13.1 us
  transfers between devices with their start and end apart: 1, of which 0 were waited for; matrix products, arithmetic and copies ran while one was open for 10% of the time, Pallas kernels for 0%

profile of v4, /device:TPU:0, one launch (start us, length us, event | category | flops | bytes accessed | tf_op | source)
XLA Modules:
  0.0 264.1 jit_solution(17789035340482726336)
XLA Ops:
  7.2 1.3 reshape_squeeze.6
  8.5 1.0 reshape_squeeze.7
  11.9 1.0 copy_bitcast_fusion.1
  15.0 1.4 fusion.3
  17.0 1.0 convert_reduce_fusion.1
  23.0 1.5 convert_element_type.56.refs_4_
  24.6 1.8 copy.54
  26.4 1.6 copy.56
  28.0 1.8 pad.5.refs_6_
  29.8 1.1 fusion.11
  30.9 1.2 divide_subtract_fusion
  33.0 1.0 constant_dynamic-slice_fusion.1
  33.9 1.0 fusion.14
  35.0 1.3 fusion.6
  38.1 2.0 copy-done.1
  40.1 1.5 copy-done.3
  41.6 1.0 copy-done.9
  43.6 15.0 %shard_map.228 = (bf16[160,384]{1,0:T(8,128)(2,1)S(1)}, bf16[160,768]{1,0:T(8,128)(2,1)S(1)}) custom-call(bf16[160,1536]{1,0:T(8,128)(2,1)S(1)} %copy-done.9, bf16[3,1536,384]{2,1,0:T(8,128)(2,1)S(1)} %bitcast.77, bf16[3,1536,384]{2,1,0:T(8,128)(2,1)S(1)} %bitcast.80, bf16[2,640,768]{2,1,0:T(8,128)(2,1)S(1)} %copy-done.3, f32[160,1]{1,0:T(8,128)S(1)} %copy-done.11, ...), custom_call_target="tpu_custom_call" | custom-call | tf_op jit(solution)/shard_map/pallas_call | solution.py:439
  58.6 57.8 %shard_map.229 = (bf16[40,1536]{1,0:T(8,128)(2,1)S(1)}, bf16[160,1536]{1,0:T(8,128)(2,1)S(1)}, f32[40,1536]{1,0:T(8,128)S(1)}) custom-call(bf16[160,384]{1,0:T(8,128)(2,1)S(1)} %get-tuple-element.18.refs_0_, f32[40,1536]{1,0:T(8,128)S(1)} %copy-done.14, f32[2,6,1536]{2,1,0:T(8,128)S(1)} %copy-done.19, f32[40,1536]{1,0:T(8,128)S(1)} %copy-done.13, ...), custom_call_target="tpu_custom_call" | custom-call | tf_op jit(solution)/shard_map/pallas_call | solution.py:312
  117.1 12.5 %shard_map.230 = (bf16[160,384]{1,0:T(8,128)(2,1)S(1)}, bf16[160,768]{1,0:T(8,128)(2,1)S(1)}) custom-call(bf16[160,1536]{1,0:T(8,128)(2,1)S(1)} %get-tuple-element.19.refs_0_, bf16[3,1536,384]{2,1,0:T(8,128)(2,1)S(1)} %bitcast.78, bf16[3,1536,384]{2,1,0:T(8,128)(2,1)S(1)} %bitcast.81, bf16[2,640,768]{2,1,0:T(8,128)(2,1)S(1)} %copy-done.4, ...), custom_call_target="tpu_custom_call" | custom-call | tf_op jit(solution)/shard_map/pallas_call | solution.py:439
  129.6 54.1 %shard_map.231 = (bf16[40,1536]{1,0:T(8,128)(2,1)S(1)}, bf16[160,1536]{1,0:T(8,128)(2,1)S(1)}, f32[40,1536]{1,0:T(8,128)S(1)}) custom-call(bf16[160,384]{1,0:T(8,128)(2,1)S(1)} %get-tuple-element.20.refs_0_, f32[40,1536]{1,0:T(8,128)S(1)} %get-tuple-element.21.refs_1_, f32[2,6,1536]{2,1,0:T(8,128)S(1)} %copy-done.17, f32[40,1536]{1,0:T(8,128)S(1)} %copy-done.12, ...), custom_call_target="tpu_custom_call" | custom-call | tf_op jit(solution)/shard_map/pallas_call | solution.py:312
  184.4 12.0 %shard_map.232 = (bf16[160,384]{1,0:T(8,128)(2,1)S(1)}, bf16[160,768]{1,0:T(8,128)(2,1)S(1)}) custom-call(bf16[160,1536]{1,0:T(8,128)(2,1)S(1)} %get-tuple-element.22.refs_0_, bf16[3,1536,384]{2,1,0:T(8,128)(2,1)S(1)} %bitcast.79, bf16[3,1536,384]{2,1,0:T(8,128)(2,1)S(1)} %bitcast.82, bf16[2,640,768]{2,1,0:T(8,128)(2,1)S(1)} %copy-done.4, ...), custom_call_target="tpu_custom_call" | custom-call | tf_op jit(solution)/shard_map/pallas_call | solution.py:439
  198.5 1.8 broadcast_in_dim_reshape.9
  201.4 54.3 %shard_map.233 = (bf16[4,16,1536]{2,1,0:T(8,128)(2,1)S(1)}, f32[4,64,128]{2,1,0:T(8,128)S(1)}) custom-call(bf16[160,384]{1,0:T(8,128)(2,1)S(1)} %copy-done.25, f32[40,1536]{1,0:T(8,128)S(1)} %copy-done.23, f32[2,6,1536]{2,1,0:T(8,128)S(1)} %copy-done.16, bf16[40,1536]{1,0:T(8,128)(2,1)S(1)} %broadcast_select_fusion.refs_3_, bf16[40,1536]{1,0:T(8,128)(2,1)S(1)} %copy-done.21, ...), custom_call_target="tpu_custom_call" | custom-call | tf_op jit(solution)/shard_map/pallas_call | solution.py:312
  (108 shorter events, 19.5 us)
Async XLA Ops:
  7.2 7.7 %copy-start.29 = (bf16[2,128,1536]{2,1,0:T(8,128)(2,1)S(1)}, bf16[2,128,1536]{2,1,0:T(8,128)(2,1)}, u32[]{:S(2)}) copy-start(bf16[2,128,1536]{2,1,0:T(8,128)(2,1)} %param.21) | copy-start | bytes 2359300
  7.2 12.2 %copy-start.32 = (s32[2,128]{1,0:T(2,128)S(1)}, s32[2,128]{1,0:T(2,128)}, u32[]{:S(2)}) copy-start(s32[2,128]{1,0:T(2,128)} %param.26) | copy-start | bytes 3076
  7.2 30.9 %all-gather.2.cloned.1.call-start = ((), (), s32[]{:S(2)}) async-start(), calls=%async_computation | async-start | bytes 2457600 | tf_op jit(solution)/shard_map/all_gather | solution.py:560
  15.0 23.1 %copy-start = (bf16[1,1536,3,384]{3,1,2,0:T(8,128)(2,1)S(1)}, bf16[1,1536,3,384]{3,1,2,0:T(8,128)(2,1)}, u32[]{:S(2)}) copy-start(bf16[1,1536,3,384]{3,1,2,0:T(8,128)(2,1)} %param.33) | copy-start | bytes 10616836
  43.5 15.0 %copy-start.5 = (bf16[1,384,1536]{2,1,0:T(8,128)(2,1)S(1)}, bf16[1,384,1536]{2,1,0:T(8,128)(2,1)}, u32[]{:S(2)}) copy-start(bf16[1,384,1536]{2,1,0:T(8,128)(2,1)} %param.34) | copy-start | bytes 3538948
  43.5 15.0 %copy-start.7 = (bf16[1,384,1536]{2,1,0:T(8,128)(2,1)S(1)}, bf16[1,384,1536]{2,1,0:T(8,128)(2,1)}, u32[]{:S(2)}) copy-start(bf16[1,384,1536]{2,1,0:T(8,128)(2,1)} %param.38) | copy-start | bytes 3538948
  43.5 15.0 %copy-start.13 = (f32[40,1536]{1,0:T(8,128)S(1)}, f32[40,1536]{1,0:T(8,128)}, u32[]{:S(2)}) copy-start(f32[40,1536]{1,0:T(8,128)} %get-tuple-element.51.refs_3_) | copy-start | bytes 737284
  43.5 15.0 %copy-start.14 = (f32[40,1536]{1,0:T(8,128)S(1)}, f32[40,1536]{1,0:T(8,128)}, u32[]{:S(2)}) copy-start(f32[40,1536]{1,0:T(8,128)} %get-tuple-element.52.refs_1_) | copy-start | bytes 737284
  43.5 15.0 %copy-start.17 = (f32[2,6,1536]{2,1,0:T(8,128)S(1)}, f32[2,6,1536]{2,1,0:T(8,128)}, u32[]{:S(2)}) copy-start(f32[2,6,1536]{2,1,0:T(8,128)} %get-tuple-element.57.refs_4_.refs_2_) | copy-start | bytes 221188
  43.6 15.0 %copy-start.19 = (f32[2,6,1536]{2,1,0:T(8,128)S(1)}, f32[2,6,1536]{2,1,0:T(8,128)}, u32[]{:S(2)}) copy-start(f32[2,6,1536]{2,1,0:T(8,128)} %copy-done.18) | copy-start | bytes 221188
  58.6 58.4 %copy-start.2 = (bf16[1,1536,3,384]{3,1,2,0:T(8,128)(2,1)S(1)}, bf16[1,1536,3,384]{3,1,2,0:T(8,128)(2,1)}, u32[]{:S(2)}) copy-start(bf16[1,1536,3,384]{3,1,2,0:T(8,128)(2,1)} %param.37) | copy-start | bytes 10616836
  58.6 58.4 %copy-start.4 = (bf16[2,640,768]{2,1,0:T(8,128)(2,1)S(1)}, bf16[2,640,768]{2,1,0:T(8,128)(2,1)}, u32[]{:S(2)}) copy-start(bf16[2,640,768]{2,1,0:T(8,128)(2,1)} %all-gather.2.cloned.1.call-done.refs_3_) | copy-start | bytes 5898244
  117.1 12.5 %copy-start.12 = (f32[40,1536]{1,0:T(8,128)S(1)}, f32[40,1536]{1,0:T(8,128)}, u32[]{:S(2)}) copy-start(f32[40,1536]{1,0:T(8,128)} %get-tuple-element.50.refs_3_) | copy-start | bytes 737284
  117.1 12.5 %copy-start.15 = (f32[2,6,1536]{2,1,0:T(8,128)S(1)}, f32[2,6,1536]{2,1,0:T(8,128)}, u32[]{:S(2)}) copy-start(f32[2,6,1536]{2,1,0:T(8,128)} %get-tuple-element.55.refs_4_.refs_2_) | copy-start | bytes 221188
  184.4 12.0 %copy-start.20 = (bf16[40,1536]{1,0:T(8,128)(2,1)}, bf16[40,1536]{1,0:T(8,128)(2,1)S(1)}, u32[]{:S(2)}) copy-start(bf16[40,1536]{1,0:T(8,128)(2,1)S(1)} %get-tuple-element.26.refs_4_) | copy-start | bytes 368644
  196.4 3.9 %copy-start.27 = (bf16[40,1536]{1,0:T(8,128)(2,1)S(1)}, bf16[40,1536]{1,0:T(8,128)(2,1)}, u32[]{:S(2)}) copy-start(bf16[40,1536]{1,0:T(8,128)(2,1)} %copy-done.26) | copy-start | bytes 368644
  196.4 4.0 %copy-start.6 = (bf16[1,384,1536]{2,1,0:T(8,128)(2,1)S(1)}, bf16[1,384,1536]{2,1,0:T(8,128)(2,1)}, u32[]{:S(2)}) copy-start(bf16[1,384,1536]{2,1,0:T(8,128)(2,1)} %param.34) | copy-start | bytes 3538948
  196.5 4.0 %copy-start.8 = (bf16[1,384,1536]{2,1,0:T(8,128)(2,1)S(1)}, bf16[1,384,1536]{2,1,0:T(8,128)(2,1)}, u32[]{:S(2)}) copy-start(bf16[1,384,1536]{2,1,0:T(8,128)(2,1)} %param.38) | copy-start | bytes 3538948
  196.5 4.0 %copy-start.10 = (bf16[1536,128]{1,0:T(8,128)(2,1)S(1)}, bf16[1536,128]{1,0:T(8,128)(2,1)}, u32[]{:S(2)}) copy-start(bf16[1536,128]{1,0:T(8,128)(2,1)} %pad.5.refs_6_) | copy-start | bytes 1179652
  196.5 4.0 %copy-start.16 = (f32[2,6,1536]{2,1,0:T(8,128)S(1)}, f32[2,6,1536]{2,1,0:T(8,128)}, u32[]{:S(2)}) copy-start(f32[2,6,1536]{2,1,0:T(8,128)} %get-tuple-element.55.refs_4_.refs_2_) | copy-start | bytes 221188
  196.5 4.0 %copy-start.23 = (f32[40,1536]{1,0:T(8,128)S(1)}, f32[40,1536]{1,0:T(8,128)}, u32[]{:S(2)}) copy-start(f32[40,1536]{1,0:T(8,128)} %copy-done.22) | copy-start | bytes 737284
  196.5 4.0 %copy-start.28 = (f32[2,2,1536]{2,1,0:T(2,128)S(1)}, f32[2,2,1536]{2,1,0:T(2,128)}, u32[]{:S(2)}) copy-start(f32[2,2,1536]{2,1,0:T(2,128)} %refs_5_.1) | copy-start | bytes 73732
  201.4 54.3 %copy-start.30 = (f32[2,128,64]{2,1,0:T(8,128)S(1)}, f32[2,128,64]{2,1,0:T(8,128)}, u32[]{:S(2)}) copy-start(f32[2,128,64]{2,1,0:T(8,128)} %copy.56) | copy-start | bytes 196612
  201.4 54.3 %copy-start.33 = (f32[2]{0:T(128)S(1)}, f32[2]{0:T(128)}, u32[]{:S(2)}) copy-start(f32[2]{0:T(128)} %get-tuple-element.49) | copy-start | bytes 28
  (11 other events, 15.9 us)
Sparse Core Ops, SparseCore 0:
  10.5 24.6 all-gather.1
